TPU v7x, 128 devices: a whole 4x4x4 slice. The times are simulated.
128 devices in a mesh: gx: 16 (over z, x_hi, core), gy: 8 (over x_lo, y).
Axes of the slice: x: 4 (x_hi: 2, x_lo: 2; x = x_hi * 2 + x_lo), y: 4, z: 4, core: 2. Of those that a mesh axis runs over, the one named last changes fastest.
Arguments:
- heights: bfloat16 [4, 1024, 4096], P(None, 'gx', 'gy'), may hold values from -6 to 6
- probes: float32 [4, 1024, 4096], P(None, 'gx', 'gy'), may hold values from -6 to 6
- cotangent: float32 [1024, 4096], P('gx', 'gy'), may hold values from -6 to 6
Outputs:
- hessian_probes: float32 [4, 1024, 4096], P(None, 'gx', 'gy')
- gradient: float32 [1024, 4096], P('gx', 'gy')
All inputs are finite; a program needn't handle non-finite values.
Results may differ from a plain program's by a relative error of at most 0.0003.
Values sent between devices are 32-bit elements; how exact they have to be, the bound alone decides.
A program may use at most 64 MiB of HBM per device.

v0:
```python
import jax
import jax.numpy as jnp
from jax import lax
from jax.sharding import PartitionSpec as P

STEPS = 4


time_step = 0.05
viscosity = 3.0
coupling = 3.0


def padded_2(x, sides, width):
    for axis, dim in sides:
        devices, length = (lax.axis_size(axis), x.shape[dim])
        up = [(i, (i + 1) % devices) for i in range(devices)]
        down = [(j, i) for i, j in up]
        last = lax.slice_in_dim(x, length - width, length, axis=dim)
        initial = lax.slice_in_dim(x, 0, width, axis=dim)
        before = lax.ppermute(last, axis, up)
        after = lax.ppermute(initial, axis, down)
        x = jnp.concatenate([before, x, after], axis=dim)
    return x


def window(padded, rim_width, margin, row_shift, col_shift):
    row_count = padded.shape[-2] - 2 * rim_width + 2 * margin
    col_count = padded.shape[-1] - 2 * rim_width + 2 * margin
    start_row = rim_width - margin + row_shift
    start_col = rim_width - margin + col_shift
    return padded[..., start_row : start_row + row_count, start_col : start_col + col_count]


def derivative_rows(padded, rim_width, margin):
    return (
        window(padded, rim_width, margin, -2, 0)
        - 8.0 * window(padded, rim_width, margin, -1, 0)
        + 8.0 * window(padded, rim_width, margin, 1, 0)
        - window(padded, rim_width, margin, 2, 0)
    ) / 12.0


def derivative_cols(padded, rim_width, margin):
    return (
        window(padded, rim_width, margin, 0, -2)
        - 8.0 * window(padded, rim_width, margin, 0, -1)
        + 8.0 * window(padded, rim_width, margin, 0, 1)
        - window(padded, rim_width, margin, 0, 2)
    ) / 12.0


def laplacian(padded, rim_width):
    rows_part = (
        -window(padded, rim_width, 0, -2, 0)
        + 16.0 * window(padded, rim_width, 0, -1, 0)
        - 30.0 * window(padded, rim_width, 0, 0, 0)
        + 16.0 * window(padded, rim_width, 0, 1, 0)
        - window(padded, rim_width, 0, 2, 0)
    ) / 12.0
    cols_part = (
        -window(padded, rim_width, 0, 0, -2)
        + 16.0 * window(padded, rim_width, 0, 0, -1)
        - 30.0 * window(padded, rim_width, 0, 0, 0)
        + 16.0 * window(padded, rim_width, 0, 0, 1)
        - window(padded, rim_width, 0, 0, 2)
    ) / 12.0
    return rows_part + cols_part


def on_device(heights, probes, cotangent):
    count_probes = probes.shape[0]
    tangent = probes
    stored = []
    for counter in range(STEPS):
        height = heights[counter].astype(jnp.float32)
        stacked = jnp.concatenate([height[None], tangent], axis=0)
        padded = padded_2(stacked, (("gx", 1), ("gy", 2)), 2)
        rim_width = 2
        margin = 0
        slope_rows = derivative_rows(padded, rim_width, margin)
        slope_cols = derivative_cols(padded, rim_width, margin)
        stored.append((slope_rows[0], slope_cols[0], slope_rows[1:], slope_cols[1:]))
        if counter + 1 < STEPS:
            diffusion = laplacian(padded[1:], rim_width)
            tangent = tangent + time_step * (
                viscosity * diffusion
                + coupling * (slope_rows[0] * slope_rows[1:] + slope_cols[0] * slope_cols[1:])
            )
    adjoint = cotangent
    second = jnp.zeros_like(probes)
    for counter in reversed(range(STEPS)):
        along_x, along_y, tangent_x, tangent_y = stored[counter]
        flux_x = adjoint * along_x
        flux_y = adjoint * along_y
        mixed_x = second * along_x + adjoint * tangent_x
        mixed_y = second * along_y + adjoint * tangent_y
        stacked = jnp.concatenate(
            [adjoint[None], second, flux_x[None], flux_y[None], mixed_x, mixed_y], axis=0
        )
        padded = padded_2(stacked, (("gx", 1), ("gy", 2)), 2)
        states = padded[: 1 + count_probes]
        padded_fx = padded[1 + count_probes]
        padded_fy = padded[2 + count_probes]
        padded_mx = padded[3 + count_probes : 3 + 2 * count_probes]
        padded_my = padded[3 + 2 * count_probes :]
        diffusion = laplacian(states, 2)
        spread_adjoint = derivative_rows(padded_fx, 2, 0) + derivative_cols(padded_fy, 2, 0)
        spread_second = derivative_rows(padded_mx, 2, 0) + derivative_cols(padded_my, 2, 0)
        new_adjoint = adjoint + time_step * (viscosity * diffusion[0] - coupling * spread_adjoint)
        second = second + time_step * (viscosity * diffusion[1:] - coupling * spread_second)
        adjoint = new_adjoint
    return (second, adjoint)


def solution(mesh):
    in_specs = (P(None, "gx", "gy"), P(None, "gx", "gy"), P("gx", "gy"))
    out_specs = (P(None, "gx", "gy"), P("gx", "gy"))
    return jax.shard_map(
        on_device, mesh=mesh, in_specs=in_specs, out_specs=out_specs, check_vma=False
    )
```

profile of v0, /device:TPU:26, one launch (start us, length us, event | category | flops | bytes accessed | tf_op | source)
XLA Modules:
  0.0 169.6 jit_solution(1770401157330916745)
XLA Ops:
  2.7 5.3 %collective-permute-start.1 = (f32[5,2,512]{2,1,0:T(2,128)S(1)}, f32[5,2,512]{2,1,0:T(2,128)S(1)}, u32[]{:S(2)}, u32[]{:S(2)}) collective-permute-start(f32[5,2,512]{2,1,0:T(2,128)S(1)} %get-tuple-element.71), channel_id=1, source_target_pairs={{8,0},{16,8},{24,16},{32,24},{40,32},{48,40},{56,48},{64,56},{72,6... | collective-permute-start | bytes 61448 | tf_op jit(solution)/shard_map/ppermute | solution.py:22
  8.0 1.5 collective-permute-done
  9.5 1.1 pad_maximum_fusion.83
  11.5 1.2 collective-permute-start.3
  13.2 4.2 %collective-permute-done.2 = f32[5,68,2]{2,1,0:T(8,128)S(1)} collective-permute-done((f32[5,68,2]{2,1,0:T(8,128)S(1)}, f32[5,68,2]{2,1,0:T(8,128)S(1)}, u32[]{:S(2)}, u32[]{:S(2)}) %collective-permute-start.2) | collective-permute-done | bytes 2752 | tf_op jit(solution)/shard_map/ppermute | solution.py:21
  17.3 2.9 %collective-permute-done.3 = f32[5,68,2]{2,1,0:T(8,128)S(1)} collective-permute-done((f32[5,68,2]{2,1,0:T(8,128)S(1)}, f32[5,68,2]{2,1,0:T(8,128)S(1)}, u32[]{:S(2)}, u32[]{:S(2)}) %collective-permute-start.3) | collective-permute-done | bytes 2752 | tf_op jit(solution)/shard_map/ppermute | solution.py:22
  22.2 5.3 %collective-permute-start.5 = (f32[5,2,512]{2,1,0:T(2,128)S(1)}, f32[5,2,512]{2,1,0:T(2,128)S(1)}, u32[]{:S(2)}, u32[]{:S(2)}) collective-permute-start(f32[5,2,512]{2,1,0:T(2,128)S(1)} %get-tuple-element.67), channel_id=1, source_target_pairs={{8,0},{16,8},{24,16},{32,24},{40,32},{48,40},{56,48},{64,56},{72,6... | collective-permute-start | bytes 61448 | tf_op jit(solution)/shard_map/ppermute | solution.py:22
  27.6 1.5 collective-permute-done.4
  29.5 1.8 %collective-permute-start.7 = (f32[5,68,2]{2,1,0:T(8,128)S(1)}, f32[5,68,2]{2,1,0:T(8,128)S(1)}, u32[]{:S(2)}, u32[]{:S(2)}) collective-permute-start(f32[5,68,2]{2,1,0:T(8,128)S(1)} %get-tuple-element.51), channel_id=1, source_target_pairs={{1,0},{2,1},{3,2},{4,3},{5,4},{6,5},{7,6},{0,7},{9,8},{10,9},{11,1... | collective-permute-start | bytes 8168 | tf_op jit(solution)/shard_map/ppermute | solution.py:22
  31.9 3.0 %collective-permute-done.6 = f32[5,68,2]{2,1,0:T(8,128)S(1)} collective-permute-done((f32[5,68,2]{2,1,0:T(8,128)S(1)}, f32[5,68,2]{2,1,0:T(8,128)S(1)}, u32[]{:S(2)}, u32[]{:S(2)}) %collective-permute-start.6) | collective-permute-done | bytes 2752 | tf_op jit(solution)/shard_map/ppermute | solution.py:21
  34.9 2.3 %collective-permute-done.7 = f32[5,68,2]{2,1,0:T(8,128)S(1)} collective-permute-done((f32[5,68,2]{2,1,0:T(8,128)S(1)}, f32[5,68,2]{2,1,0:T(8,128)S(1)}, u32[]{:S(2)}, u32[]{:S(2)}) %collective-permute-start.7) | collective-permute-done | bytes 2752 | tf_op jit(solution)/shard_map/ppermute | solution.py:22
  39.2 5.3 %collective-permute-start.9 = (f32[5,2,512]{2,1,0:T(2,128)S(1)}, f32[5,2,512]{2,1,0:T(2,128)S(1)}, u32[]{:S(2)}, u32[]{:S(2)}) collective-permute-start(f32[5,2,512]{2,1,0:T(2,128)S(1)} %get-tuple-element.63), channel_id=1, source_target_pairs={{8,0},{16,8},{24,16},{32,24},{40,32},{48,40},{56,48},{64,56},{72,6... | collective-permute-start | bytes 61448 | tf_op jit(solution)/shard_map/ppermute | solution.py:22
  44.6 1.6 collective-permute-done.8
  46.4 2.0 %collective-permute-start.11 = (f32[5,68,2]{2,1,0:T(8,128)S(1)}, f32[5,68,2]{2,1,0:T(8,128)S(1)}, u32[]{:S(2)}, u32[]{:S(2)}) collective-permute-start(f32[5,68,2]{2,1,0:T(8,128)S(1)} %get-tuple-element.47), channel_id=1, source_target_pairs={{1,0},{2,1},{3,2},{4,3},{5,4},{6,5},{7,6},{0,7},{9,8},{10,9},{11,1... | collective-permute-start | bytes 8168 | tf_op jit(solution)/shard_map/ppermute | solution.py:22
  48.9 3.0 %collective-permute-done.10 = f32[5,68,2]{2,1,0:T(8,128)S(1)} collective-permute-done((f32[5,68,2]{2,1,0:T(8,128)S(1)}, f32[5,68,2]{2,1,0:T(8,128)S(1)}, u32[]{:S(2)}, u32[]{:S(2)}) %collective-permute-start.10) | collective-permute-done | bytes 2752 | tf_op jit(solution)/shard_map/ppermute | solution.py:21
  51.9 2.2 %collective-permute-done.11 = f32[5,68,2]{2,1,0:T(8,128)S(1)} collective-permute-done((f32[5,68,2]{2,1,0:T(8,128)S(1)}, f32[5,68,2]{2,1,0:T(8,128)S(1)}, u32[]{:S(2)}, u32[]{:S(2)}) %collective-permute-start.11) | collective-permute-done | bytes 2752 | tf_op jit(solution)/shard_map/ppermute | solution.py:22
  56.2 5.3 %collective-permute-start.13 = (f32[5,2,512]{2,1,0:T(2,128)S(1)}, f32[5,2,512]{2,1,0:T(2,128)S(1)}, u32[]{:S(2)}, u32[]{:S(2)}) collective-permute-start(f32[5,2,512]{2,1,0:T(2,128)S(1)} %get-tuple-element.59), channel_id=1, source_target_pairs={{8,0},{16,8},{24,16},{32,24},{40,32},{48,40},{56,48},{64,56},{72,6... | collective-permute-start | bytes 61448 | tf_op jit(solution)/shard_map/ppermute | solution.py:22
  61.6 1.4 collective-permute-done.12
  63.3 2.0 %collective-permute-start.15 = (f32[5,68,2]{2,1,0:T(8,128)S(1)}, f32[5,68,2]{2,1,0:T(8,128)S(1)}, u32[]{:S(2)}, u32[]{:S(2)}) collective-permute-start(f32[5,68,2]{2,1,0:T(8,128)S(1)} %get-tuple-element.43), channel_id=1, source_target_pairs={{1,0},{2,1},{3,2},{4,3},{5,4},{6,5},{7,6},{0,7},{9,8},{10,9},{11,1... | collective-permute-start | bytes 8168 | tf_op jit(solution)/shard_map/ppermute | solution.py:22
  65.8 3.0 %collective-permute-done.14 = f32[5,68,2]{2,1,0:T(8,128)S(1)} collective-permute-done((f32[5,68,2]{2,1,0:T(8,128)S(1)}, f32[5,68,2]{2,1,0:T(8,128)S(1)}, u32[]{:S(2)}, u32[]{:S(2)}) %collective-permute-start.14) | collective-permute-done | bytes 2752 | tf_op jit(solution)/shard_map/ppermute | solution.py:21
  68.8 2.9 %collective-permute-done.15 = f32[5,68,2]{2,1,0:T(8,128)S(1)} collective-permute-done((f32[5,68,2]{2,1,0:T(8,128)S(1)}, f32[5,68,2]{2,1,0:T(8,128)S(1)}, u32[]{:S(2)}, u32[]{:S(2)}) %collective-permute-start.15) | collective-permute-done | bytes 2752 | tf_op jit(solution)/shard_map/ppermute | solution.py:22
  73.0 5.3 %collective-permute-start.17 = (f32[15,2,512]{2,1,0:T(2,128)S(1)}, f32[15,2,512]{2,1,0:T(2,128)S(1)}, u32[]{:S(2)}, u32[]{:S(2)}) collective-permute-start(f32[15,2,512]{2,1,0:T(2,128)S(1)} %get-tuple-element.39), channel_id=1, source_target_pairs={{8,0},{16,8},{24,16},{32,24},{40,32},{48,40},{56,48},{64,56},{72,6... | collective-permute-start | bytes 184328 | tf_op jit(solution)/shard_map/ppermute | solution.py:22
  79.0 1.2 collective-permute-done.16
  81.9 1.3 copy.19
  83.5 4.1 %collective-permute-start.18 = (f32[15,68,2]{1,2,0:T(2,128)S(1)}, f32[15,68,2]{1,2,0:T(2,128)S(1)}, u32[]{:S(2)}, u32[]{:S(2)}) collective-permute-start(f32[15,68,2]{1,2,0:T(2,128)S(1)} %copy.19), channel_id=1, source_target_pairs={{0,1},{1,2},{2,3},{3,4},{4,5},{5,6},{6,7},{7,0},{8,9},{9,10},{10,1... | collective-permute-start | bytes 24488 | tf_op jit(solution)/shard_map/ppermute | solution.py:21
  93.0 1.6 broadcast_multiply_fusion
  95.7 5.3 %collective-permute-start.21 = (f32[15,2,512]{2,1,0:T(2,128)S(1)}, f32[15,2,512]{2,1,0:T(2,128)S(1)}, u32[]{:S(2)}, u32[]{:S(2)}) collective-permute-start(f32[15,2,512]{2,1,0:T(2,128)S(1)} %get-tuple-element.37), channel_id=1, source_target_pairs={{8,0},{16,8},{24,16},{32,24},{40,32},{48,40},{56,48},{64,56},{72,6... | collective-permute-start | bytes 184328 | tf_op jit(solution)/shard_map/ppermute | solution.py:22
  101.1 2.1 %collective-permute-done.20 = f32[15,2,512]{2,1,0:T(2,128)S(1)} collective-permute-done((f32[15,2,512]{2,1,0:T(2,128)S(1)}, f32[15,2,512]{2,1,0:T(2,128)S(1)}, u32[]{:S(2)}, u32[]{:S(2)}) %collective-permute-start.20) | collective-permute-done | bytes 61472 | tf_op jit(solution)/shard_map/ppermute | solution.py:21
  104.3 1.4 copy.25
  105.7 4.8 %collective-permute-start.22 = (f32[15,68,2]{1,2,0:T(2,128)S(1)}, f32[15,68,2]{1,2,0:T(2,128)S(1)}, u32[]{:S(2)}, u32[]{:S(2)}) collective-permute-start(f32[15,68,2]{1,2,0:T(2,128)S(1)} %copy.25), channel_id=1, source_target_pairs={{0,1},{1,2},{2,3},{3,4},{4,5},{5,6},{6,7},{7,0},{8,9},{9,10},{10,1... | collective-permute-start | bytes 24488 | tf_op jit(solution)/shard_map/ppermute | solution.py:21
  112.2 4.6 %collective-permute-done.23 = f32[15,68,2]{1,2,0:T(2,128)S(1)} collective-permute-done((f32[15,68,2]{1,2,0:T(2,128)S(1)}, f32[15,68,2]{1,2,0:T(2,128)S(1)}, u32[]{:S(2)}, u32[]{:S(2)}) %collective-permute-start.23) | collective-permute-done | bytes 8192 | tf_op jit(solution)/shard_map/ppermute | solution.py:22
  120.7 1.9 %constant_dynamic-update-slice_fusion.3 = (f32[15,64,512]{2,1,0:T(8,128)S(1)}, f32[4,64,512]{2,1,0:T(8,128)S(1)}) fusion(f32[15,64,512]{2,1,0:T(8,128)S(1)} %get-tuple-element.10, f32[15,68,2]{2,1,0:T(8,128)S(1)} %copy-done.8, f32[15,2,512]{2,1,0:T(2,128)} %copy-done.32, f32[15,64,512]{2,1,0:T(8,128)S(1)} %copy-done.4, ...), kind=kLoop, calls=%fused_computation.515 | loop fusion | flops 4325376 | bytes 4747232
  123.8 5.3 %collective-permute-start.25 = (f32[15,2,512]{2,1,0:T(2,128)S(1)}, f32[15,2,512]{2,1,0:T(2,128)S(1)}, u32[]{:S(2)}, u32[]{:S(2)}) collective-permute-start(f32[15,2,512]{2,1,0:T(2,128)S(1)} %get-tuple-element.35), channel_id=1, source_target_pairs={{8,0},{16,8},{24,16},{32,24},{40,32},{48,40},{56,48},{64,56},{72,6... | collective-permute-start | bytes 184328 | tf_op jit(solution)/shard_map/ppermute | solution.py:22
  129.2 1.9 %collective-permute-done.24 = f32[15,2,512]{2,1,0:T(2,128)S(1)} collective-permute-done((f32[15,2,512]{2,1,0:T(2,128)S(1)}, f32[15,2,512]{2,1,0:T(2,128)S(1)}, u32[]{:S(2)}, u32[]{:S(2)}) %collective-permute-start.24) | collective-permute-done | bytes 61472 | tf_op jit(solution)/shard_map/ppermute | solution.py:21
  131.1 1.2 pad_maximum_fusion.13
  132.3 1.3 copy.31
  133.7 1.3 copy.33
  135.0 2.1 %collective-permute-start.27 = (f32[15,68,2]{1,2,0:T(2,128)S(1)}, f32[15,68,2]{1,2,0:T(2,128)S(1)}, u32[]{:S(2)}, u32[]{:S(2)}) collective-permute-start(f32[15,68,2]{1,2,0:T(2,128)S(1)} %copy.33), channel_id=1, source_target_pairs={{1,0},{2,1},{3,2},{4,3},{5,4},{6,5},{7,6},{0,7},{9,8},{10,9},{11,1... | collective-permute-start | bytes 24488 | tf_op jit(solution)/shard_map/ppermute | solution.py:22
  138.5 2.4 %collective-permute-done.27 = f32[15,68,2]{1,2,0:T(2,128)S(1)} collective-permute-done((f32[15,68,2]{1,2,0:T(2,128)S(1)}, f32[15,68,2]{1,2,0:T(2,128)S(1)}, u32[]{:S(2)}, u32[]{:S(2)}) %collective-permute-start.27) | collective-permute-done | bytes 8192 | tf_op jit(solution)/shard_map/ppermute | solution.py:22
  142.0 1.1 maximum_bitcast_fusion.1
  144.6 1.6 constant_dynamic-update-slice_fusion.5
  147.4 5.3 %collective-permute-start.29 = (f32[15,2,512]{2,1,0:T(2,128)S(1)}, f32[15,2,512]{2,1,0:T(2,128)S(1)}, u32[]{:S(2)}, u32[]{:S(2)}) collective-permute-start(f32[15,2,512]{2,1,0:T(2,128)S(1)} %get-tuple-element.33), channel_id=1, source_target_pairs={{8,0},{16,8},{24,16},{32,24},{40,32},{48,40},{56,48},{64,56},{72,6... | collective-permute-start | bytes 184328 | tf_op jit(solution)/shard_map/ppermute | solution.py:22
  152.8 2.1 %collective-permute-done.28 = f32[15,2,512]{2,1,0:T(2,128)S(1)} collective-permute-done((f32[15,2,512]{2,1,0:T(2,128)S(1)}, f32[15,2,512]{2,1,0:T(2,128)S(1)}, u32[]{:S(2)}, u32[]{:S(2)}) %collective-permute-start.28) | collective-permute-done | bytes 61472 | tf_op jit(solution)/shard_map/ppermute | solution.py:21
  155.9 1.4 copy.37
  157.7 2.3 %collective-permute-start.31 = (f32[15,68,2]{1,2,0:T(2,128)S(1)}, f32[15,68,2]{1,2,0:T(2,128)S(1)}, u32[]{:S(2)}, u32[]{:S(2)}) collective-permute-start(f32[15,68,2]{1,2,0:T(2,128)S(1)} %copy.39), channel_id=1, source_target_pairs={{1,0},{2,1},{3,2},{4,3},{5,4},{6,5},{7,6},{0,7},{9,8},{10,9},{11,1... | collective-permute-start | bytes 24488 | tf_op jit(solution)/shard_map/ppermute | solution.py:22
  160.0 1.1 collective-permute-done.30
  161.4 2.4 %collective-permute-done.31 = f32[15,68,2]{1,2,0:T(2,128)S(1)} collective-permute-done((f32[15,68,2]{1,2,0:T(2,128)S(1)}, f32[15,68,2]{1,2,0:T(2,128)S(1)}, u32[]{:S(2)}, u32[]{:S(2)}) %collective-permute-start.31) | collective-permute-done | bytes 8192 | tf_op jit(solution)/shard_map/ppermute | solution.py:22
  168.0 1.6 fusion.96
  (191 shorter events, 40.7 us)
Async XLA Ops:
  0.6 12.1 %copy-start.5 = (f32[4,64,512]{2,1,0:T(8,128)S(1)}, f32[4,64,512]{2,1,0:T(8,128)}, u32[]{:S(2)}) copy-start(f32[4,64,512]{2,1,0:T(8,128)} %param.4) | copy-start | bytes 1572868
  2.6 6.9 %collective-permute-start = (f32[5,2,512]{2,1,0:T(2,128)S(1)}, f32[5,2,512]{2,1,0:T(2,128)S(1)}, u32[]{:S(2)}, u32[]{:S(2)}) collective-permute-start(f32[5,2,512]{2,1,0:T(2,128)S(1)} %get-tuple-element.70), channel_id=1, source_target_pairs={{0,8},{8,16},{16,24},{24,32},{32,40},{40,48},{48,56},{56,64},{64,7... | collective-permute-start | bytes 61448 | tf_op jit(solution)/shard_map/ppermute | solution.py:21
  2.7 6.8 %collective-permute-start.1 = (f32[5,2,512]{2,1,0:T(2,128)S(1)}, f32[5,2,512]{2,1,0:T(2,128)S(1)}, u32[]{:S(2)}, u32[]{:S(2)}) collective-permute-start(f32[5,2,512]{2,1,0:T(2,128)S(1)} %get-tuple-element.71), channel_id=1, source_target_pairs={{8,0},{16,8},{24,16},{32,24},{40,32},{48,40},{56,48},{64,56},{72,6... | collective-permute-start | bytes 61448 | tf_op jit(solution)/shard_map/ppermute | solution.py:22
  10.6 6.7 %collective-permute-start.2 = (f32[5,68,2]{2,1,0:T(8,128)S(1)}, f32[5,68,2]{2,1,0:T(8,128)S(1)}, u32[]{:S(2)}, u32[]{:S(2)}) collective-permute-start(f32[5,68,2]{2,1,0:T(8,128)S(1)} %get-tuple-element.54), channel_id=1, source_target_pairs={{0,1},{1,2},{2,3},{3,4},{4,5},{5,6},{6,7},{7,0},{8,9},{9,10},{10,1... | collective-permute-start | bytes 8168 | tf_op jit(solution)/shard_map/ppermute | solution.py:21
  11.5 8.7 %collective-permute-start.3 = (f32[5,68,2]{2,1,0:T(8,128)S(1)}, f32[5,68,2]{2,1,0:T(8,128)S(1)}, u32[]{:S(2)}, u32[]{:S(2)}) collective-permute-start(f32[5,68,2]{2,1,0:T(8,128)S(1)} %get-tuple-element.55), channel_id=1, source_target_pairs={{1,0},{2,1},{3,2},{4,3},{5,4},{6,5},{7,6},{0,7},{9,8},{10,9},{11,1... | collective-permute-start | bytes 8168 | tf_op jit(solution)/shard_map/ppermute | solution.py:22
  13.1 8.1 %copy-start.17 = (f32[5,64,512]{2,1,0:T(8,128)}, f32[5,64,512]{2,1,0:T(8,128)S(1)}, u32[]{:S(2)}) copy-start(f32[5,64,512]{2,1,0:T(8,128)S(1)} %fusion.85) | copy-start | bytes 1966084
  22.1 6.9 %collective-permute-start.4 = (f32[5,2,512]{2,1,0:T(2,128)S(1)}, f32[5,2,512]{2,1,0:T(2,128)S(1)}, u32[]{:S(2)}, u32[]{:S(2)}) collective-permute-start(f32[5,2,512]{2,1,0:T(2,128)S(1)} %get-tuple-element.66), channel_id=1, source_target_pairs={{0,8},{8,16},{16,24},{24,32},{32,40},{40,48},{48,56},{56,64},{64,7... | collective-permute-start | bytes 61448 | tf_op jit(solution)/shard_map/ppermute | solution.py:21
  22.2 6.9 %collective-permute-start.5 = (f32[5,2,512]{2,1,0:T(2,128)S(1)}, f32[5,2,512]{2,1,0:T(2,128)S(1)}, u32[]{:S(2)}, u32[]{:S(2)}) collective-permute-start(f32[5,2,512]{2,1,0:T(2,128)S(1)} %get-tuple-element.67), channel_id=1, source_target_pairs={{8,0},{16,8},{24,16},{32,24},{40,32},{48,40},{56,48},{64,56},{72,6... | collective-permute-start | bytes 61448 | tf_op jit(solution)/shard_map/ppermute | solution.py:22
  29.3 5.6 %collective-permute-start.6 = (f32[5,68,2]{2,1,0:T(8,128)S(1)}, f32[5,68,2]{2,1,0:T(8,128)S(1)}, u32[]{:S(2)}, u32[]{:S(2)}) collective-permute-start(f32[5,68,2]{2,1,0:T(8,128)S(1)} %get-tuple-element.50), channel_id=1, source_target_pairs={{0,1},{1,2},{2,3},{3,4},{4,5},{5,6},{6,7},{7,0},{8,9},{9,10},{10,1... | collective-permute-start | bytes 8168 | tf_op jit(solution)/shard_map/ppermute | solution.py:21
  29.5 7.6 %collective-permute-start.7 = (f32[5,68,2]{2,1,0:T(8,128)S(1)}, f32[5,68,2]{2,1,0:T(8,128)S(1)}, u32[]{:S(2)}, u32[]{:S(2)}) collective-permute-start(f32[5,68,2]{2,1,0:T(8,128)S(1)} %get-tuple-element.51), channel_id=1, source_target_pairs={{1,0},{2,1},{3,2},{4,3},{5,4},{6,5},{7,6},{0,7},{9,8},{10,9},{11,1... | collective-permute-start | bytes 8168 | tf_op jit(solution)/shard_map/ppermute | solution.py:22
  31.8 6.4 %copy-start.21 = (f32[5,64,512]{2,1,0:T(8,128)}, f32[5,64,512]{2,1,0:T(8,128)S(1)}, u32[]{:S(2)}) copy-start(f32[5,64,512]{2,1,0:T(8,128)S(1)} %fusion.79) | copy-start | bytes 1966084
  31.9 6.4 %copy-start.28 = (f32[64,512]{1,0:T(8,128)}, f32[64,512]{1,0:T(8,128)S(1)}, u32[]{:S(2)}) copy-start(f32[64,512]{1,0:T(8,128)S(1)} %slice_bitcast_fusion.5) | copy-start | bytes 393220
  38.3 6.3 %copy-start.16 = (f32[64,512]{1,0:T(8,128)S(1)}, f32[64,512]{1,0:T(8,128)}, u32[]{:S(2)}) copy-start(f32[64,512]{1,0:T(8,128)} %param.5) | copy-start | bytes 393220
  39.1 7.0 %collective-permute-start.8 = (f32[5,2,512]{2,1,0:T(2,128)S(1)}, f32[5,2,512]{2,1,0:T(2,128)S(1)}, u32[]{:S(2)}, u32[]{:S(2)}) collective-permute-start(f32[5,2,512]{2,1,0:T(2,128)S(1)} %get-tuple-element.62), channel_id=1, source_target_pairs={{0,8},{8,16},{16,24},{24,32},{32,40},{40,48},{48,56},{56,64},{64,7... | collective-permute-start | bytes 61448 | tf_op jit(solution)/shard_map/ppermute | solution.py:21
  39.2 7.0 %collective-permute-start.9 = (f32[5,2,512]{2,1,0:T(2,128)S(1)}, f32[5,2,512]{2,1,0:T(2,128)S(1)}, u32[]{:S(2)}, u32[]{:S(2)}) collective-permute-start(f32[5,2,512]{2,1,0:T(2,128)S(1)} %get-tuple-element.63), channel_id=1, source_target_pairs={{8,0},{16,8},{24,16},{32,24},{40,32},{48,40},{56,48},{64,56},{72,6... | collective-permute-start | bytes 61448 | tf_op jit(solution)/shard_map/ppermute | solution.py:22
  46.3 5.6 %collective-permute-start.10 = (f32[5,68,2]{2,1,0:T(8,128)S(1)}, f32[5,68,2]{2,1,0:T(8,128)S(1)}, u32[]{:S(2)}, u32[]{:S(2)}) collective-permute-start(f32[5,68,2]{2,1,0:T(8,128)S(1)} %get-tuple-element.46), channel_id=1, source_target_pairs={{0,1},{1,2},{2,3},{3,4},{4,5},{5,6},{6,7},{7,0},{8,9},{9,10},{10,1... | collective-permute-start | bytes 8168 | tf_op jit(solution)/shard_map/ppermute | solution.py:21
  46.4 7.7 %collective-permute-start.11 = (f32[5,68,2]{2,1,0:T(8,128)S(1)}, f32[5,68,2]{2,1,0:T(8,128)S(1)}, u32[]{:S(2)}, u32[]{:S(2)}) collective-permute-start(f32[5,68,2]{2,1,0:T(8,128)S(1)} %get-tuple-element.47), channel_id=1, source_target_pairs={{1,0},{2,1},{3,2},{4,3},{5,4},{6,5},{7,6},{0,7},{9,8},{10,9},{11,1... | collective-permute-start | bytes 8168 | tf_op jit(solution)/shard_map/ppermute | solution.py:22
  48.8 29.5 %copy-start.12 = (f32[5,64,512]{2,1,0:T(8,128)}, f32[5,64,512]{2,1,0:T(8,128)S(1)}, u32[]{:S(2)}) copy-start(f32[5,64,512]{2,1,0:T(8,128)S(1)} %fusion.73) | copy-start | bytes 1966084
  55.1 32.6 %copy-start.14 = (f32[5,64,512]{2,1,0:T(8,128)}, f32[5,64,512]{2,1,0:T(8,128)S(1)}, u32[]{:S(2)}) copy-start(f32[5,64,512]{2,1,0:T(8,128)S(1)} %fusion.70) | copy-start | bytes 1966084
  55.9 7.1 %collective-permute-start.12 = (f32[5,2,512]{2,1,0:T(2,128)S(1)}, f32[5,2,512]{2,1,0:T(2,128)S(1)}, u32[]{:S(2)}, u32[]{:S(2)}) collective-permute-start(f32[5,2,512]{2,1,0:T(2,128)S(1)} %get-tuple-element.58), channel_id=1, source_target_pairs={{0,8},{8,16},{16,24},{24,32},{32,40},{40,48},{48,56},{56,64},{64,7... | collective-permute-start | bytes 61448 | tf_op jit(solution)/shard_map/ppermute | solution.py:21
  56.2 6.8 %collective-permute-start.13 = (f32[5,2,512]{2,1,0:T(2,128)S(1)}, f32[5,2,512]{2,1,0:T(2,128)S(1)}, u32[]{:S(2)}, u32[]{:S(2)}) collective-permute-start(f32[5,2,512]{2,1,0:T(2,128)S(1)} %get-tuple-element.59), channel_id=1, source_target_pairs={{8,0},{16,8},{24,16},{32,24},{40,32},{48,40},{56,48},{64,56},{72,6... | collective-permute-start | bytes 61448 | tf_op jit(solution)/shard_map/ppermute | solution.py:22
  63.2 5.6 %collective-permute-start.14 = (f32[5,68,2]{2,1,0:T(8,128)S(1)}, f32[5,68,2]{2,1,0:T(8,128)S(1)}, u32[]{:S(2)}, u32[]{:S(2)}) collective-permute-start(f32[5,68,2]{2,1,0:T(8,128)S(1)} %get-tuple-element.42), channel_id=1, source_target_pairs={{0,1},{1,2},{2,3},{3,4},{4,5},{5,6},{6,7},{7,0},{8,9},{9,10},{10,1... | collective-permute-start | bytes 8168 | tf_op jit(solution)/shard_map/ppermute | solution.py:21
  63.3 8.4 %collective-permute-start.15 = (f32[5,68,2]{2,1,0:T(8,128)S(1)}, f32[5,68,2]{2,1,0:T(8,128)S(1)}, u32[]{:S(2)}, u32[]{:S(2)}) collective-permute-start(f32[5,68,2]{2,1,0:T(8,128)S(1)} %get-tuple-element.43), channel_id=1, source_target_pairs={{1,0},{2,1},{3,2},{4,3},{5,4},{6,5},{7,6},{0,7},{9,8},{10,9},{11,1... | collective-permute-start | bytes 8168 | tf_op jit(solution)/shard_map/ppermute | solution.py:22
  72.9 7.3 %collective-permute-start.16 = (f32[15,2,512]{2,1,0:T(2,128)S(1)}, f32[15,2,512]{2,1,0:T(2,128)S(1)}, u32[]{:S(2)}, u32[]{:S(2)}) collective-permute-start(f32[15,2,512]{2,1,0:T(2,128)S(1)} %get-tuple-element.38), channel_id=1, source_target_pairs={{0,8},{8,16},{16,24},{24,32},{32,40},{40,48},{48,56},{56,64},{64,7... | collective-permute-start | bytes 184328 | tf_op jit(solution)/shard_map/ppermute | solution.py:21
  73.0 7.2 %collective-permute-start.17 = (f32[15,2,512]{2,1,0:T(2,128)S(1)}, f32[15,2,512]{2,1,0:T(2,128)S(1)}, u32[]{:S(2)}, u32[]{:S(2)}) collective-permute-start(f32[15,2,512]{2,1,0:T(2,128)S(1)} %get-tuple-element.39), channel_id=1, source_target_pairs={{8,0},{16,8},{24,16},{32,24},{40,32},{48,40},{56,48},{64,56},{72,6... | collective-permute-start | bytes 184328 | tf_op jit(solution)/shard_map/ppermute | solution.py:22
  83.5 5.9 %collective-permute-start.19 = (f32[15,68,2]{1,2,0:T(2,128)S(1)}, f32[15,68,2]{1,2,0:T(2,128)S(1)}, u32[]{:S(2)}, u32[]{:S(2)}) collective-permute-start(f32[15,68,2]{1,2,0:T(2,128)S(1)} %copy.21), channel_id=1, source_target_pairs={{1,0},{2,1},{3,2},{4,3},{5,4},{6,5},{7,6},{0,7},{9,8},{10,9},{11,1... | collective-permute-start | bytes 24488 | tf_op jit(solution)/shard_map/ppermute | solution.py:22
  83.5 5.6 %collective-permute-start.18 = (f32[15,68,2]{1,2,0:T(2,128)S(1)}, f32[15,68,2]{1,2,0:T(2,128)S(1)}, u32[]{:S(2)}, u32[]{:S(2)}) collective-permute-start(f32[15,68,2]{1,2,0:T(2,128)S(1)} %copy.19), channel_id=1, source_target_pairs={{0,1},{1,2},{2,3},{3,4},{4,5},{5,6},{6,7},{7,0},{8,9},{9,10},{10,1... | collective-permute-start | bytes 24488 | tf_op jit(solution)/shard_map/ppermute | solution.py:21
  89.4 2.2 %copy-start.34 = (f32[15,2,512]{2,1,0:T(2,128)S(1)}, f32[15,2,512]{2,1,0:T(2,128)}, u32[]{:S(2)}) copy-start(f32[15,2,512]{2,1,0:T(2,128)} %copy-done.33) | copy-start | bytes 184324
  95.6 7.6 %copy-start.2 = (f32[15,64,512]{2,1,0:T(8,128)}, f32[15,64,512]{2,1,0:T(8,128)S(1)}, u32[]{:S(2)}) copy-start(f32[15,64,512]{2,1,0:T(8,128)S(1)} %add_dynamic-update-slice_fusion.4) | copy-start | bytes 5898244
  95.6 7.5 %collective-permute-start.20 = (f32[15,2,512]{2,1,0:T(2,128)S(1)}, f32[15,2,512]{2,1,0:T(2,128)S(1)}, u32[]{:S(2)}, u32[]{:S(2)}) collective-permute-start(f32[15,2,512]{2,1,0:T(2,128)S(1)} %get-tuple-element.36), channel_id=1, source_target_pairs={{0,8},{8,16},{16,24},{24,32},{32,40},{40,48},{48,56},{56,64},{64,7... | collective-permute-start | bytes 184328 | tf_op jit(solution)/shard_map/ppermute | solution.py:21
  95.7 7.5 %collective-permute-start.21 = (f32[15,2,512]{2,1,0:T(2,128)S(1)}, f32[15,2,512]{2,1,0:T(2,128)S(1)}, u32[]{:S(2)}, u32[]{:S(2)}) collective-permute-start(f32[15,2,512]{2,1,0:T(2,128)S(1)} %get-tuple-element.37), channel_id=1, source_target_pairs={{8,0},{16,8},{24,16},{32,24},{40,32},{48,40},{56,48},{64,56},{72,6... | collective-permute-start | bytes 184328 | tf_op jit(solution)/shard_map/ppermute | solution.py:22
  103.2 15.8 %copy-start.32 = (f32[15,2,512]{2,1,0:T(2,128)}, f32[15,2,512]{2,1,0:T(2,128)S(1)}, u32[]{:S(2)}) copy-start(f32[15,2,512]{2,1,0:T(2,128)S(1)} %collective-permute-done.21) | copy-start | bytes 184324
  104.3 13.6 %copy-start.3 = (f32[15,64,512]{2,1,0:T(8,128)S(1)}, f32[15,64,512]{2,1,0:T(8,128)}, u32[]{:S(2)}) copy-start(f32[15,64,512]{2,1,0:T(8,128)} %copy-done.2) | copy-start | bytes 5898244
  105.7 6.2 %collective-permute-start.22 = (f32[15,68,2]{1,2,0:T(2,128)S(1)}, f32[15,68,2]{1,2,0:T(2,128)S(1)}, u32[]{:S(2)}, u32[]{:S(2)}) collective-permute-start(f32[15,68,2]{1,2,0:T(2,128)S(1)} %copy.25), channel_id=1, source_target_pairs={{0,1},{1,2},{2,3},{3,4},{4,5},{5,6},{6,7},{7,0},{8,9},{9,10},{10,1... | collective-permute-start | bytes 24488 | tf_op jit(solution)/shard_map/ppermute | solution.py:21
  110.7 6.1 %collective-permute-start.23 = (f32[15,68,2]{1,2,0:T(2,128)S(1)}, f32[15,68,2]{1,2,0:T(2,128)S(1)}, u32[]{:S(2)}, u32[]{:S(2)}) collective-permute-start(f32[15,68,2]{1,2,0:T(2,128)S(1)} %copy.27), channel_id=1, source_target_pairs={{1,0},{2,1},{3,2},{4,3},{5,4},{6,5},{7,6},{0,7},{9,8},{10,9},{11,1... | collective-permute-start | bytes 24488 | tf_op jit(solution)/shard_map/ppermute | solution.py:22
  112.2 6.8 %copy-start.6 = (f32[15,68,2]{2,1,0:T(8,128)}, f32[15,68,2]{2,1,0:T(8,128)S(1)}, u32[]{:S(2)}) copy-start(f32[15,68,2]{2,1,0:T(8,128)S(1)} %copy.26) | copy-start | bytes 24484
  120.7 2.0 %copy-start.29 = (f32[64,512]{1,0:T(8,128)S(1)}, f32[64,512]{1,0:T(8,128)}, u32[]{:S(2)}) copy-start(f32[64,512]{1,0:T(8,128)} %copy-done.28) | copy-start | bytes 393220
  123.8 7.3 %collective-permute-start.24 = (f32[15,2,512]{2,1,0:T(2,128)S(1)}, f32[15,2,512]{2,1,0:T(2,128)S(1)}, u32[]{:S(2)}, u32[]{:S(2)}) collective-permute-start(f32[15,2,512]{2,1,0:T(2,128)S(1)} %get-tuple-element.34), channel_id=1, source_target_pairs={{0,8},{8,16},{16,24},{24,32},{32,40},{40,48},{48,56},{56,64},{64,7... | collective-permute-start | bytes 184328 | tf_op jit(solution)/shard_map/ppermute | solution.py:21
  123.8 7.2 %collective-permute-start.25 = (f32[15,2,512]{2,1,0:T(2,128)S(1)}, f32[15,2,512]{2,1,0:T(2,128)S(1)}, u32[]{:S(2)}, u32[]{:S(2)}) collective-permute-start(f32[15,2,512]{2,1,0:T(2,128)S(1)} %get-tuple-element.35), channel_id=1, source_target_pairs={{8,0},{16,8},{24,16},{32,24},{40,32},{48,40},{56,48},{64,56},{72,6... | collective-permute-start | bytes 184328 | tf_op jit(solution)/shard_map/ppermute | solution.py:22
  131.1 12.0 %copy-start.36 = (f32[15,2,512]{2,1,0:T(2,128)}, f32[15,2,512]{2,1,0:T(2,128)S(1)}, u32[]{:S(2)}) copy-start(f32[15,2,512]{2,1,0:T(2,128)S(1)} %collective-permute-done.25) | copy-start | bytes 184324
  133.6 3.8 %collective-permute-start.26 = (f32[15,68,2]{1,2,0:T(2,128)S(1)}, f32[15,68,2]{1,2,0:T(2,128)S(1)}, u32[]{:S(2)}, u32[]{:S(2)}) collective-permute-start(f32[15,68,2]{1,2,0:T(2,128)S(1)} %copy.31), channel_id=1, source_target_pairs={{0,1},{1,2},{2,3},{3,4},{4,5},{5,6},{6,7},{7,0},{8,9},{9,10},{10,1... | collective-permute-start | bytes 24488 | tf_op jit(solution)/shard_map/ppermute | solution.py:21
  135.0 5.9 %collective-permute-start.27 = (f32[15,68,2]{1,2,0:T(2,128)S(1)}, f32[15,68,2]{1,2,0:T(2,128)S(1)}, u32[]{:S(2)}, u32[]{:S(2)}) collective-permute-start(f32[15,68,2]{1,2,0:T(2,128)S(1)} %copy.33), channel_id=1, source_target_pairs={{1,0},{2,1},{3,2},{4,3},{5,4},{6,5},{7,6},{0,7},{9,8},{10,9},{11,1... | collective-permute-start | bytes 24488 | tf_op jit(solution)/shard_map/ppermute | solution.py:22
  147.3 7.6 %copy-start = (f32[15,64,512]{2,1,0:T(8,128)}, f32[15,64,512]{2,1,0:T(8,128)S(1)}, u32[]{:S(2)}) copy-start(f32[15,64,512]{2,1,0:T(8,128)S(1)} %add_dynamic-update-slice_fusion) | copy-start | bytes 5898244
  147.3 7.5 %collective-permute-start.28 = (f32[15,2,512]{2,1,0:T(2,128)S(1)}, f32[15,2,512]{2,1,0:T(2,128)S(1)}, u32[]{:S(2)}, u32[]{:S(2)}) collective-permute-start(f32[15,2,512]{2,1,0:T(2,128)S(1)} %get-tuple-element.32), channel_id=1, source_target_pairs={{0,8},{8,16},{16,24},{24,32},{32,40},{40,48},{48,56},{56,64},{64,7... | collective-permute-start | bytes 184328 | tf_op jit(solution)/shard_map/ppermute | solution.py:21
  147.4 7.4 %collective-permute-start.29 = (f32[15,2,512]{2,1,0:T(2,128)S(1)}, f32[15,2,512]{2,1,0:T(2,128)S(1)}, u32[]{:S(2)}, u32[]{:S(2)}) collective-permute-start(f32[15,2,512]{2,1,0:T(2,128)S(1)} %get-tuple-element.33), channel_id=1, source_target_pairs={{8,0},{16,8},{24,16},{32,24},{40,32},{48,40},{56,48},{64,56},{72,6... | collective-permute-start | bytes 184328 | tf_op jit(solution)/shard_map/ppermute | solution.py:22
  155.9 9.0 %copy-start.1 = (f32[15,64,512]{2,1,0:T(8,128)S(1)}, f32[15,64,512]{2,1,0:T(8,128)}, u32[]{:S(2)}) copy-start(f32[15,64,512]{2,1,0:T(8,128)} %copy-done) | copy-start | bytes 5898244
  157.4 3.8 %collective-permute-start.30 = (f32[15,68,2]{1,2,0:T(2,128)S(1)}, f32[15,68,2]{1,2,0:T(2,128)S(1)}, u32[]{:S(2)}, u32[]{:S(2)}) collective-permute-start(f32[15,68,2]{1,2,0:T(2,128)S(1)} %copy.37), channel_id=1, source_target_pairs={{0,1},{1,2},{2,3},{3,4},{4,5},{5,6},{6,7},{7,0},{8,9},{9,10},{10,1... | collective-permute-start | bytes 24488 | tf_op jit(solution)/shard_map/ppermute | solution.py:21
  157.7 6.2 %collective-permute-start.31 = (f32[15,68,2]{1,2,0:T(2,128)S(1)}, f32[15,68,2]{1,2,0:T(2,128)S(1)}, u32[]{:S(2)}, u32[]{:S(2)}) collective-permute-start(f32[15,68,2]{1,2,0:T(2,128)S(1)} %copy.39), channel_id=1, source_target_pairs={{1,0},{2,1},{3,2},{4,3},{5,4},{6,5},{7,6},{0,7},{9,8},{10,9},{11,1... | collective-permute-start | bytes 24488 | tf_op jit(solution)/shard_map/ppermute | solution.py:22
  (23 other events, 29.0 us)
where the time goes:
time: 170 us
  starting transfers between devices  65.7 us (39%)
  waiting for transfers between devices  49.5 us (29%)
  other arithmetic  35.5 us (21%)
  local copies, waits for them, and re-layouts  17.4 us (10%)
    ppermute x16, starting transfers between devices, padded_2(): after = lax.ppermute(initial, axis, down)  54.6 us
    ppermute x16, waiting for transfers between devices, padded_2(): before = lax.ppermute(last, axis, up)  29.7 us
    ppermute x16, waiting for transfers between devices, padded_2(): after = lax.ppermute(initial, axis, down)  19.8 us
    ppermute x16, starting transfers between devices, padded_2(): before = lax.ppermute(last, axis, up)  11.1 us
    slice x12, other arithmetic, padded_2(): last = lax.slice_in_dim(x, length - width, length, axis=dim)  6.89 us
    slice x8, local copies, waits for them, and re-layouts, padded_2(): last = lax.slice_in_dim(x, length - width, length, axis=dim)  5.63 us
    unnamed x18, other arithmetic  5.2 us
    ppermute x4, local copies, waits for them, and re-layouts, padded_2(): after = lax.ppermute(initial, axis, down)  4.33 us
  transfers between devices with their start and end apart: 32, of which 24 were waited for; matrix products, arithmetic and copies ran while one was open for 4% of the time, Pallas kernels for 0%

commit v1 on v0

v1 whole, which is shorter than its diff:
```python
import functools

import jax
import jax.numpy as jnp
from jax import lax
from jax.experimental import pallas as pl
from jax.experimental.pallas import tpu as pltpu
from jax.sharding import PartitionSpec as P

STEPS = 4
PROBES = 4
TILES = 5
REACH = 16
ROWS, COLS = 64, 512
SPAN = ROWS + 2 * REACH

time_step = 0.05
viscosity = 3.0
coupling = 3.0
A = time_step * viscosity / 12.0
KEEP = 1.0 - 60.0 * A
SLOPE = 1.0 / 12.0

WIDTHS = [16] * PROBES + [16, 14, 12, 10] + [8]
LANES = [sum(WIDTHS[:f]) for f in range(len(WIDTHS))]
PACK_ROWS = [0, 16, 30, 42, 52]
MESH = pl.DeviceIdType.MESH


def left(x, by):
    return pltpu.roll(x, by % 128, 1)


def lanes(rows):
    return lax.broadcasted_iota(jnp.int32, (rows, 128), 1)


def kernel(
    heights, probes, cotangent, q_out, p_out,
    hb, ub, cb, send_rows, rows_u, rows_h, send_cols, cols,
    H, U0, U1, U2, U3, AR, AC, BR, BC, PP, MP, M3, N3, Q3, Q2, QR, Q1, M2, M1, M0,
    local_sem, send_sem, recv_sem, far_sem,
):
    gx, gy = lax.axis_index("gx"), lax.axis_index("gy")
    n_gx, n_gy = lax.axis_size("gx"), lax.axis_size("gy")
    core = lax.rem(gx, 2)
    late = lax.rem(lax.div(gx, 2), 2)
    near_gx = gx + 1 - 2 * core
    far_gx = lax.rem(gx - 1 + 2 * core + n_gx, n_gx)
    west, east = lax.rem(gy + n_gy - 1, n_gy), lax.rem(gy + 1, n_gy)
    near_group = [(near_gx, gy), (gx, west), (gx, east), (near_gx, west), (near_gx, east)]
    far_group = [(far_gx, gy), (far_gx, west), (far_gx, east)]

    loads = [
        pltpu.make_async_copy(heights, hb, local_sem.at[0]),
        pltpu.make_async_copy(cotangent, cb, local_sem.at[1]),
        pltpu.make_async_copy(probes, ub, local_sem.at[2]),
    ]
    for c in loads:
        c.start()

    barrier = pltpu.get_barrier_semaphore()
    for d in near_group:
        pl.semaphore_signal(barrier, inc=1, device_id=d, device_id_type=MESH)

    near_edge, far_edge = 1 - core, core
    near_halo, far_halo = 1 - core, core

    def copy(src, dst, s, d):
        return pltpu.make_async_remote_copy(
            src_ref=src, dst_ref=dst, send_sem=send_sem.at[s], recv_sem=recv_sem.at[s],
            device_id=d, device_id_type=MESH,
        )

    def row_start(edge):
        return pl.multiple_of(edge * (ROWS - REACH), 16)

    def halo_start(halo):
        return pl.multiple_of(halo * (SPAN - REACH), 16)

    def u_copy(edge, p, s, d):
        return copy(probes.at[p, pl.ds(row_start(edge), REACH)], rows_u.at[1 - edge, p], s, d)

    def h_copy(edge, s, d):
        part = (slice(None), pl.ds(0, 64))
        return copy(send_rows.at[(edge, *part)], rows_h.at[(1 - edge, *part)], s, d)

    def c_copy(side, s, d):
        return copy(send_cols.at[side], cols.at[1 - side, pl.ds(REACH, ROWS)], s, d)

    def k_copy(side, edge, s, d):
        return copy(
            send_cols.at[side, pl.ds(row_start(edge), REACH)],
            cols.at[1 - side, pl.ds(halo_start(1 - edge), REACH)], s, d,
        )

    far_u = [u_copy(far_edge, p, p, far_group[0]) for p in range(PROBES)]
    far_h = h_copy(far_edge, 4, far_group[0])
    far_k = [k_copy(0, far_edge, 5, far_group[1]), k_copy(1, far_edge, 6, far_group[2])]
    near_u = [u_copy(near_edge, p, 7 + p, near_group[0]) for p in range(PROBES)]
    near_h = h_copy(near_edge, 11, near_group[0])
    near_k = [k_copy(0, near_edge, 12, near_group[3]), k_copy(1, near_edge, 13, near_group[4])]
    side_c = [c_copy(0, 14, near_group[1]), c_copy(1, 15, near_group[2])]

    @pl.when(late == 0)
    def _():
        pl.semaphore_wait(barrier, 5)
        for d in far_group:
            pl.semaphore_signal(barrier, inc=1, device_id=d, device_id_type=MESH)

    @pl.when(late == 1)
    def _():
        pl.semaphore_wait(barrier, 8)
        for c in far_u:
            c.start()
        for d in far_group:
            pl.semaphore_signal(far_sem, inc=1, device_id=d, device_id_type=MESH)

    for c in near_u:
        c.start()

    loads[0].wait()
    loads[1].wait()
    for n in range(4):
        cut = slice(128 * n, 128 * n + 128)
        for k in range(STEPS):
            send_rows[0, n, PACK_ROWS[k] : PACK_ROWS[k] + 16] = hb[k, 0:16, cut].astype(jnp.float32)
        send_rows[0, n, 52:60] = cb[0:8, cut]
        for k in reversed(range(STEPS)):
            first = PACK_ROWS[k] - 2 * k
            send_rows[1, n, first : first + 16] = hb[k, 48:64, cut].astype(jnp.float32)
        send_rows[1, n, 52:60] = cb[56:64, cut]
    near_h.start()

    @pl.when(late == 1)
    def _():
        far_h.start()

    loads[2].wait()
    lane = lanes(ROWS)
    for side in (0, 1):
        packed = None
        for f, (w, o) in enumerate(zip(WIDTHS, LANES)):
            cut = slice(0, 128) if side == 0 else slice(COLS - 128, COLS)
            if f < 4:
                x = ub[f, :, cut]
            elif f < 8:
                x = hb[f - 4, :, cut].astype(jnp.float32)
            else:
                x = cb[:, cut]
            x = left(x, o if side == 0 else o + w)
            packed = x if packed is None else jnp.where(lane < o, packed, x)
        send_cols[side] = packed
    for c in side_c + near_k:
        c.start()

    @pl.when(late == 1)
    def _():
        for c in far_k:
            c.start()

    def to_tiles(store, nat, before, after, f, rows):
        lane = lanes(rows)
        w, o = WIDTHS[f], LANES[f]
        store(0, jnp.where(lane < 16, left(before, 16 - w - o), left(nat[0], 16)))
        for j, (shift) in ((1, 40), (2, 64), (3, 88)):
            store(j, jnp.where(lane < shift, left(nat[j - 1], shift), left(nat[j], shift)))
        store(4, jnp.where(lane < 112, left(nat[3], 112), left(after, 112 - o)))

    def put(ref, lead, start, rows):
        def store(j, value):
            ref[(*lead, j, pl.ds(start, rows))] = value

        return store

    def load_own():
        before, after = cols[0, REACH : REACH + ROWS], cols[1, REACH : REACH + ROWS]
        for f in range(9):
            if f < 4:
                nat, dst = [ub[f, :, 128 * n : 128 * n + 128] for n in range(4)], put(U0, (f,), REACH, ROWS)
            elif f < 8:
                nat = [hb[f - 4, :, 128 * n : 128 * n + 128].astype(jnp.float32) for n in range(4)]
                dst = put(H, (f - 4,), REACH, ROWS)
            else:
                nat, dst = [cb[:, 128 * n : 128 * n + 128] for n in range(4)], put(PP, (4,), REACH, ROWS)
            to_tiles(dst, nat, before, after, f, ROWS)

    def load_halo(halo, fields):
        start = halo_start(halo)
        before, after = cols[0, pl.ds(start, REACH)], cols[1, pl.ds(start, REACH)]
        for f in fields:
            if f < 4:
                nat = [rows_u[halo, f, :, 128 * n : 128 * n + 128] for n in range(4)]
                dst = put(U0, (f,), start, REACH)
            else:
                k = f - 4
                shift = 2 * k
                first = PACK_ROWS[k] - (1 - halo) * shift
                nat = [rows_h[halo, n, pl.ds(first, REACH)] for n in range(4)]
                dst = put(H, (k,), start, REACH) if f < 8 else put(PP, (4,), start, REACH)
            to_tiles(dst, nat, before, after, f, REACH)

    def slopes(region):
        def body(k, _):
            start, rows = region(k)
            for j in range(TILES):
                at = lambda d: H[k, j, pl.ds(start + d, rows)]
                x = at(0)
                AR[k, j, pl.ds(start, rows)] = SLOPE * (8.0 * (at(1) - at(-1)) - (at(2) - at(-2)))
                AC[k, j, pl.ds(start, rows)] = SLOPE * (
                    8.0 * (left(x, -1) - left(x, 1)) - (left(x, -2) - left(x, 2))
                )
            return 0

        lax.fori_loop(0, STEPS, body, 0)

    def over(first, last, batch, body):
        if last - first == batch:
            for i in range(batch):
                body(first + i)
            return

        def step(i, _):
            for b in range(batch):
                body(first + i * batch + b)
            return 0

        lax.fori_loop(0, (last - first) // batch, step, 0)

    def tangent(k, source, target, region):
        start, rows = region

        def body(p):
            for j in range(TILES):
                here = pl.ds(start, rows)
                at = lambda d: source[p, j, pl.ds(start + d, rows)]
                x, n1, s1, n2, s2 = at(0), at(-1), at(1), at(-2), at(2)
                w1, e1, w2, e2 = left(x, 1), left(x, -1), left(x, 2), left(x, -2)
                br = 8.0 * (s1 - n1) - (s2 - n2)
                bc = 8.0 * (e1 - w1) - (e2 - w2)
                if target is None:
                    adjoint = SLOPE * PP[STEPS, j, here]
                    M3[p, j, here] = adjoint * br
                    N3[p, j, here] = adjoint * bc
                    continue
                BR[k, p, j, here] = SLOPE * br
                BC[k, p, j, here] = SLOPE * bc
                lap = 16.0 * ((n1 + s1) + (w1 + e1)) - ((n2 + s2) + (w2 + e2))
                target[p, j, here] = KEEP * x + A * (
                    lap + AR[k, j, here] * br + AC[k, j, here] * bc
                )

        return body

    def spread(q_at, m_at, my):
        x = q_at(0)
        two = x + x
        ring = left(two + my, 1) + left(two - my, -1)
        s = q_at(-1) + q_at(1)
        ring = ring + ((s + s) + (m_at(-1) - m_at(1)))
        outer = left(x + my, 2) + left(x - my, -2)
        outer = outer + ((q_at(-2) + q_at(2)) + (m_at(-2) - m_at(2)))
        return KEEP * x + A * (8.0 * ring - outer)

    def p_flux(region):
        start, rows = region
        here = pl.ds(start, rows)
        for j in range(TILES):
            MP[STEPS, j, here] = PP[STEPS, j, here] * AR[STEPS - 1, j, here]

    def p_step(k, region):
        start, rows = region
        here = pl.ds(start, rows)
        results = []
        for j in range(TILES):
            q_at = lambda d: PP[k + 1, j, pl.ds(start + d, rows)]
            m_at = lambda d: MP[k + 1, j, pl.ds(start + d, rows)]
            out = spread(q_at, m_at, q_at(0) * AC[k, j, here])
            if k > 0:
                PP[k, j, here] = out
                MP[k, j, here] = out * AR[k - 1, j, here]
            results.append(out)
        if k == 0:
            to_natural(p_out, (), results, start, rows)

    def to_natural(ref, lead, tiles, start, rows):
        lane = lanes(rows)
        moved = [left(t, s) for t, s in zip(tiles, (112, 88, 64, 40, 16))]
        first = pl.multiple_of(start - REACH, 16)
        for n, edge in enumerate((100, 76, 52, 28)):
            ref[(*lead, pl.ds(first, rows), slice(128 * n, 128 * n + 128))] = jnp.where(
                lane < edge, moved[n], moved[n + 1]
            )

    def q_first(region):
        start, rows = region

        def body(p):
            here = pl.ds(start, rows)
            for j in range(TILES):
                m_at = lambda d: M3[p, j, pl.ds(start + d, rows)]
                my = N3[p, j, here]
                ring = (left(my, 1) - left(my, -1)) + (m_at(-1) - m_at(1))
                outer = (left(my, 2) - left(my, -2)) + (m_at(-2) - m_at(2))
                out = A * (8.0 * ring - outer)
                Q3[p, j, here] = out
                M2[p, j, here] = out * AR[2, j, here] + PP[3, j, here] * BR[2, p, j, here]

        return body

    def q_step(k, source, flux, target, next_flux, region):
        start, rows = region

        def body(p):
            here = pl.ds(start, rows)
            results = []
            for j in range(TILES):
                q_at = lambda d: source[p, j, pl.ds(start + d, rows)]
                m_at = lambda d: flux[p, j, pl.ds(start + d, rows)]
                my = q_at(0) * AC[k, j, here] + PP[k + 1, j, here] * BC[k, p, j, here]
                out = spread(q_at, m_at, my)
                if target is not None:
                    target[p, j, here] = out
                if next_flux is not None:
                    next_flux[p, j, here] = out * AR[k - 1, j, here] + PP[k, j, here] * BR[k - 1, p, j, here]
                results.append(out)
            if target is None:
                to_natural(q_out, (p,), results, start, rows)

        return body

    def refresh(region):
        start, rows = region

        def body(p):
            here = pl.ds(start, rows)
            lane = lanes(rows)
            for j in range(TILES):
                x = Q2[p, j, here]
                if j > 0:
                    x = jnp.where(lane < 12, left(Q2[p, j - 1, here], -104), x)
                if j < TILES - 1:
                    x = jnp.where(lane >= 116, left(Q2[p, j + 1, here], 104), x)
                QR[p, j, here] = x
                M1[p, j, here] = x * AR[1, j, here] + PP[2, j, here] * BR[1, p, j, here]

        return body

    def shared(region):
        slopes(lambda k: region(2, k))
        p_flux(region(8))
        for k in reversed(range(STEPS)):
            p_step(k, region(16 - 2 * k))

    def sweep(region, first, last, batch):
        run = functools.partial(over, first, last, batch)
        run(tangent(0, U0, U1, region(2)))
        run(tangent(1, U1, U2, region(4)))
        run(tangent(2, U2, U3, region(6)))
        run(tangent(3, U3, None, region(8)))
        run(q_first(region(10)))
        run(q_step(2, Q3, M2, Q2, None, region(12)))
        run(refresh(region(12)))
        run(q_step(1, QR, M1, Q1, M0, region(14)))
        run(q_step(0, Q1, M0, None, None, region(16)))

    def main_region(margin, k=None):
        rows = (80 - 2 * margin + 7) // 8 * 8
        if margin == 16:
            return pl.multiple_of(32 - 16 * core, 16), rows
        return (1 - core) * (SPAN - margin - rows) + core * margin, rows

    for c in near_u + [near_h] + near_k + side_c:
        c.wait_recv()
    load_own()
    load_halo(near_halo, range(9))

    @pl.when(late == 0)
    def _():
        pl.semaphore_wait(far_sem, 3)
        for c in far_u + [far_h] + far_k:
            c.start()

    shared(main_region)
    sweep(main_region, 0, PROBES, 2)

    def wedge_region(margin, k=None):
        if margin == 16:
            return pl.multiple_of(16 + 48 * core, 16), REACH
        m = margin if k is None else 2 * k + 2
        return (1 - core) * m + core * (80 - m), REACH

    far_h.wait_recv()
    for c in far_k:
        c.wait_recv()
    load_halo(far_halo, range(4, 9))
    shared(wedge_region)
    for first in (0, 2):
        for p in (first, first + 1):
            far_u[p].wait_recv()
        load_halo(far_halo, (first, first + 1))
        sweep(wedge_region, first, first + 2, 2)

    for c in far_u + [far_h] + far_k + near_u + [near_h] + near_k + side_c:
        c.wait_send()


def on_device(heights, probes, cotangent):
    f32 = jnp.float32
    probe = pltpu.VMEM((PROBES, TILES, SPAN, 128), f32)
    return pl.pallas_call(
        kernel,
        out_shape=[
            jax.ShapeDtypeStruct((PROBES, ROWS, COLS), f32),
            jax.ShapeDtypeStruct((ROWS, COLS), f32),
        ],
        in_specs=[pl.BlockSpec(memory_space=pl.ANY)] * 3,
        out_specs=[pl.BlockSpec(memory_space=pltpu.VMEM)] * 2,
        scratch_shapes=[
            pltpu.VMEM((STEPS, ROWS, COLS), jnp.bfloat16),
            pltpu.VMEM((PROBES, ROWS, COLS), f32),
            pltpu.VMEM((ROWS, COLS), f32),
            pltpu.VMEM((2, 4, 72, 128), f32),
            pltpu.VMEM((2, PROBES, REACH, COLS), f32),
            pltpu.VMEM((2, 4, 72, 128), f32),
            pltpu.VMEM((2, ROWS, 128), f32),
            pltpu.VMEM((2, SPAN, 128), f32),
            probe,
            probe, probe, probe, probe,
            probe, probe,
            pltpu.VMEM((3, PROBES, TILES, SPAN, 128), f32),
            pltpu.VMEM((3, PROBES, TILES, SPAN, 128), f32),
            pltpu.VMEM((STEPS + 1, TILES, SPAN, 128), f32),
            pltpu.VMEM((STEPS + 1, TILES, SPAN, 128), f32),
            probe, probe, probe, probe, probe, probe, probe, probe, probe,
            pltpu.SemaphoreType.DMA((3,)),
            pltpu.SemaphoreType.DMA((16,)),
            pltpu.SemaphoreType.DMA((16,)),
            pltpu.SemaphoreType.REGULAR,
        ],
        compiler_params=pltpu.CompilerParams(
            collective_id=0, has_side_effects=True, vmem_limit_bytes=56 * 2**20
        ),
    )(heights, probes, cotangent)


def solution(mesh):
    in_specs = (P(None, "gx", "gy"), P(None, "gx", "gy"), P("gx", "gy"))
    out_specs = (P(None, "gx", "gy"), P("gx", "gy"))
    return jax.shard_map(
        on_device, mesh=mesh, in_specs=in_specs, out_specs=out_specs, check_vma=False
    )
```

time: 170 us -> 35.6 us (0.21)
  the two profiles are of different devices: /device:TPU:26 before, /device:TPU:4 now
where the time goes in v1:
time: 35.6 us; the launch traced here: 35.5 us
  Pallas kernels  32.3 us (91%)
  local copies, waits for them, and re-layouts  2.56 us (7%)
  between operations  0.65 us (2%)
    pallas_call x1, Pallas kernels, on_device(): pl.pallas_call(kernel, out_shape=[jax.ShapeDtypeStruct((PROBES, ROWS, COL...  32.3 us
    unnamed x4, local copies, waits for them, and re-layouts  2.56 us

profile of v1, /device:TPU:4, one launch (start us, length us, event | category | flops | bytes accessed | tf_op | source)
XLA Modules:
  0.0 35.5 jit_solution(5030969781492888039)
XLA Ops:
  0.6 32.3 %shard_map.50 = (f32[4,64,512]{2,1,0:T(8,128)}, f32[64,512]{1,0:T(8,128)}) custom-call(bf16[4,64,512]{2,1,0:T(8,128)(2,1)} %heights.1, f32[4,64,512]{2,1,0:T(8,128)} %probes.1, f32[64,512]{1,0:T(8,128)} %cotangent.1), custom_call_target="tpu_custom_call" | custom-call | tf_op jit(solution)/shard_map/pallas_call | solution.py:411
  32.9 0.0 copy-start
  32.9 1.9 %copy.7 = f32[4,64,512]{2,1,0:T(8,128)} copy(f32[4,64,512]{2,1,0:T(8,128)} %get-tuple-element.4) | data formatting | bytes 1048576
  34.8 0.0 copy-done
  34.8 0.7 %copy.8 = f32[64,512]{1,0:T(8,128)} copy(f32[64,512]{1,0:T(8,128)S(1)} %copy-done) | data formatting | bytes 262144
Async XLA Ops:
  32.9 1.9 %copy-start = (f32[64,512]{1,0:T(8,128)S(1)}, f32[64,512]{1,0:T(8,128)}, u32[]{:S(2)}) copy-start(f32[64,512]{1,0:T(8,128)} %get-tuple-element.5) | copy-start | bytes 393220

commit v2 on v1

v2 whole, which is shorter than its diff:
```python
import functools

import jax
import jax.numpy as jnp
from jax import lax
from jax.experimental import pallas as pl
from jax.experimental.pallas import tpu as pltpu
from jax.sharding import PartitionSpec as P

STEPS = 4
PROBES = 4
TILES = 5
REACH = 16
ROWS, COLS = 64, 512
SPAN = ROWS + 2 * REACH

time_step = 0.05
viscosity = 3.0
coupling = 3.0
A = time_step * viscosity / 12.0
KEEP = 1.0 - 60.0 * A
SLOPE = 1.0 / 12.0

WIDTHS = [16] * PROBES + [16, 14, 12, 10] + [8]
LANES = [sum(WIDTHS[:f]) for f in range(len(WIDTHS))]
PACK_ROWS = [0, 16, 30, 42, 52]
MESH = pl.DeviceIdType.MESH


def left(x, by):
    return pltpu.roll(x, by % 128, 1)


def lanes(rows):
    return lax.broadcasted_iota(jnp.int32, (rows, 128), 1)


def kernel(
    heights, probes, cotangent, q_out, p_out,
    hb, ub, cb, send_rows, rows_u, rows_h, send_cols, cols,
    H, U0, U1, U2, U3, AR, AC, BR, BC, PP, PS, MP, M3, N3, Q3, Q2, QR, Q1, M2, M1, M0, W, WK,
    local_sem, send_sem, recv_sem, answer,
):
    gx, gy = lax.axis_index("gx"), lax.axis_index("gy")
    n_gx, n_gy = lax.axis_size("gx"), lax.axis_size("gy")
    core = lax.rem(gx, 2)
    late = lax.rem(lax.div(gx, 2), 2)
    near_gx = gx + 1 - 2 * core
    far_gx = lax.rem(gx - 1 + 2 * core + n_gx, n_gx)
    west, east = lax.rem(gy + n_gy - 1, n_gy), lax.rem(gy + 1, n_gy)
    y = lax.rem(gy, 4)

    def signal(sem, device):
        pl.semaphore_signal(sem, inc=1, device_id=device, device_id_type=MESH)

    greets_far, greets_near, greets_west, greets_east = late == 0, core == 1, y == 0, y < 3
    barrier = pltpu.get_barrier_semaphore()
    far_corners = [(far_gx, west), (far_gx, east)]

    @pl.when(greets_near)
    def _():
        signal(barrier, (near_gx, gy))

    @pl.when(greets_far)
    def _():
        for d in [(far_gx, gy)] + far_corners:
            signal(barrier, d)

    @pl.when(greets_east)
    def _():
        for d in [(gx, east), (near_gx, east)]:
            signal(barrier, d)

    @pl.when(greets_west)
    def _():
        for d in [(gx, west), (near_gx, west)]:
            signal(barrier, d)

    loads = [
        pltpu.make_async_copy(heights, hb, local_sem.at[0]),
        pltpu.make_async_copy(cotangent, cb, local_sem.at[1]),
        pltpu.make_async_copy(probes, ub, local_sem.at[2]),
    ]
    for c in loads:
        c.start()

    def taps(rows, one, two, sign):
        into = lax.broadcasted_iota(jnp.int32, (rows, 128), 0)
        off = lax.rem(into, 128) - lax.broadcasted_iota(jnp.int32, (rows, 128), 1)
        value = jnp.where(off == 1, one, 0.0) + jnp.where(off == -1, sign * one, 0.0)
        value = value + jnp.where(off == 2, two, 0.0) + jnp.where(off == -2, sign * two, 0.0)
        return value.astype(jnp.bfloat16)

    W[:, 0:128] = taps(256, 8.0, -1.0, -1.0)
    W[:, 128:256] = taps(256, 16.0, -1.0, 1.0)
    WK[0:256] = taps(256, 16.0, -1.0, 1.0)
    WK[256:512] = taps(256, -8.0, 1.0, -1.0)

    near_edge, far_edge = 1 - core, core
    near_halo, far_halo = 1 - core, core

    def copy(src, dst, s, d):
        return pltpu.make_async_remote_copy(
            src_ref=src, dst_ref=dst, send_sem=send_sem.at[s], recv_sem=recv_sem.at[s],
            device_id=d, device_id_type=MESH,
        )

    def row_start(edge):
        return pl.multiple_of(edge * (ROWS - REACH), 16)

    def halo_start(halo):
        return pl.multiple_of(halo * (SPAN - REACH), 16)

    def u_copy(edge, p, s, d):
        return copy(probes.at[p, pl.ds(row_start(edge), REACH)], rows_u.at[1 - edge, p], s, d)

    def h_copy(edge, s, d):
        part = (slice(None), pl.ds(0, 64))
        return copy(send_rows.at[(edge, *part)], rows_h.at[(1 - edge, *part)], s, d)

    def c_copy(side, s, d):
        return copy(send_cols.at[side], cols.at[1 - side, pl.ds(REACH, ROWS)], s, d)

    def k_copy(side, edge, s, d):
        return copy(
            send_cols.at[side, pl.ds(row_start(edge), REACH)],
            cols.at[1 - side, pl.ds(halo_start(1 - edge), REACH)], s, d,
        )

    far_u = [u_copy(far_edge, p, p, (far_gx, gy)) for p in range(PROBES)]
    far_h = h_copy(far_edge, 4, (far_gx, gy))
    far_k = [k_copy(side, far_edge, 5 + side, far_corners[side]) for side in (0, 1)]
    near_u = [u_copy(near_edge, p, 7 + p, (near_gx, gy)) for p in range(PROBES)]
    near_h = h_copy(near_edge, 11, (near_gx, gy))
    near_k = [k_copy(0, near_edge, 12, (near_gx, west)), k_copy(1, near_edge, 13, (near_gx, east))]
    side_c = [c_copy(0, 14, (gx, west)), c_copy(1, 15, (gx, east))]

    greeters = 3 * late + (1 - core) + jnp.where(y > 0, 2, 0) + jnp.where(y == 3, 2, 0)

    @pl.when(greeters > 0)
    def _():
        pl.semaphore_wait(barrier, greeters)


    @pl.when(late == 1)
    def _():
        for c in far_u[:2]:
            c.start()
        signal(answer.at[0], (far_gx, gy))
        for d in far_corners:
            signal(answer.at[1], d)

    @pl.when(core == 0)
    def _():
        signal(answer.at[2], (near_gx, gy))

    @pl.when(y > 0)
    def _():
        for d in [(gx, west), (near_gx, west)]:
            signal(answer.at[4], d)

    @pl.when(y == 3)
    def _():
        for d in [(gx, east), (near_gx, east)]:
            signal(answer.at[3], d)

    def answered(greeted, which, count):
        @pl.when(greeted)
        def _():
            pl.semaphore_wait(answer.at[which], count)

    def early_sends():
        pl.semaphore_wait(answer.at[0], 1)
        for c in far_u[:2] + [far_h] + far_u[2:]:
            c.start()
        pl.semaphore_wait(answer.at[1], 2)
        for c in far_k:
            c.start()

    answered(greets_near, 2, 1)
    for c in near_u:
        c.start()

    loads[0].wait()
    loads[1].wait()
    for n in range(4):
        cut = slice(128 * n, 128 * n + 128)
        for k in range(STEPS):
            send_rows[0, n, PACK_ROWS[k] : PACK_ROWS[k] + 16] = hb[k, 0:16, cut].astype(jnp.float32)
        send_rows[0, n, 52:60] = cb[0:8, cut]
        for k in reversed(range(STEPS)):
            first = PACK_ROWS[k] - 2 * k
            send_rows[1, n, first : first + 16] = hb[k, 48:64, cut].astype(jnp.float32)
        send_rows[1, n, 52:60] = cb[56:64, cut]
    near_h.start()

    loads[2].wait()
    lane = lanes(ROWS)
    for side in (0, 1):
        packed = None
        for f, (w, o) in enumerate(zip(WIDTHS, LANES)):
            cut = slice(0, 128) if side == 0 else slice(COLS - 128, COLS)
            if f < 4:
                x = ub[f, :, cut]
            elif f < 8:
                x = hb[f - 4, :, cut].astype(jnp.float32)
            else:
                x = cb[:, cut]
            x = left(x, o if side == 0 else o + w)
            packed = x if packed is None else jnp.where(lane < o, packed, x)
        send_cols[side] = packed
    for side, greeted in ((0, greets_west), (1, greets_east)):
        answered(greeted, 3 + side, 2)
        for c in (side_c[side], near_k[side]):
            c.start()

    @pl.when(late == 1)
    def _():
        for c in far_k + [far_h] + far_u[2:]:
            c.start()

    def inner_tiles(store, nat, rows):
        lane = lanes(rows)
        for j, shift in ((1, 40), (2, 64), (3, 88)):
            store(j, jnp.where(lane < shift, left(nat[j - 1], shift), left(nat[j], shift)))
        return left(nat[0], 16), left(nat[3], 112)

    def outer_tiles(store, first, last, before, after, f, rows):
        lane = lanes(rows)
        w, o = WIDTHS[f], LANES[f]
        store(0, jnp.where(lane < 16, left(before, 16 - w - o), first))
        store(4, jnp.where(lane < 112, last, left(after, 112 - o)))

    def place(f):
        return (U0, (f,)) if f < 4 else (H, (f - 4,)) if f < 8 else (PP, (4,))

    def put(f, start, rows):
        ref, lead = place(f)

        def store(j, value):
            ref[(*lead, j, pl.ds(start, rows))] = value

        return store

    def load_own():
        for f in range(9):
            cuts = [slice(128 * n, 128 * n + 128) for n in range(4)]
            if f < 4:
                nat = [ub[f, :, cut] for cut in cuts]
            elif f < 8:
                nat = [hb[f - 4, :, cut].astype(jnp.float32) for cut in cuts]
            else:
                nat = [cb[:, cut] for cut in cuts]
            store = put(f, REACH, ROWS)
            first, last = inner_tiles(store, nat, ROWS)
            store(0, first)
            store(4, last)

    def own_sides():
        before, after = cols[0, REACH : REACH + ROWS], cols[1, REACH : REACH + ROWS]
        for f in range(9):
            ref, lead = place(f)
            mine = slice(REACH, REACH + ROWS)
            outer_tiles(put(f, REACH, ROWS), ref[(*lead, 0, mine)], ref[(*lead, 4, mine)], before, after, f, ROWS)

    def load_halo(halo, fields):
        start = halo_start(halo)
        before, after = cols[0, pl.ds(start, REACH)], cols[1, pl.ds(start, REACH)]
        for f in fields:
            if f < 4:
                nat = [rows_u[halo, f, :, 128 * n : 128 * n + 128] for n in range(4)]
            else:
                k = f - 4
                first = PACK_ROWS[k] - (1 - halo) * (2 * k)
                nat = [rows_h[halo, n, pl.ds(first, REACH)] for n in range(4)]
            store = put(f, start, REACH)
            first, last = inner_tiles(store, nat, REACH)
            outer_tiles(store, first, last, before, after, f, REACH)

    def dot(x, w):
        return jnp.dot(x, w, preferred_element_type=jnp.float32)

    def halves(x):
        high = x.astype(jnp.bfloat16)
        return [high, (x - high.astype(jnp.float32)).astype(jnp.bfloat16)]

    def along(columns, w):
        rows = columns[0][0].shape[0]
        stacked = [jnp.concatenate(sum([halves(x) for x in xs], []), axis=1) for xs in columns]
        out = dot(jnp.concatenate(stacked, axis=0), w)
        return [out[i * rows : i * rows + rows] for i in range(len(columns))]

    def slopes(region):
        for k in range(STEPS):
            start, rows = region(2 * k + 2)
            here = pl.ds(start, rows)
            whole = jnp.concatenate([H[k, j, here].astype(jnp.bfloat16) for j in range(TILES)], axis=0)
            cross = dot(whole, W[0:128, 0:128])
            for j in range(TILES):
                at = lambda d: H[k, j, pl.ds(start + d, rows)]
                AR[k, j, here] = SLOPE * (8.0 * (at(1) - at(-1)) - (at(2) - at(-2)))
                AC[k, j, here] = SLOPE * cross[j * rows : j * rows + rows]

    def over(first, last, batch, body):
        pairs = [(p, j) for p in range(first, last) for j in range(TILES)]
        for i in range(0, len(pairs), batch):
            body(pairs[i : i + batch])

    def tangent(k, source, target, region):
        start, rows = region
        here = pl.ds(start, rows)

        def body(pairs):
            cross = along([[source[p, j, here]] for p, j in pairs], W[:, 0:128] if target is None else W[...])
            for (p, j), c in zip(pairs, cross):
                at = lambda d: source[p, j, pl.ds(start + d, rows)]
                n1, s1, n2, s2 = at(-1), at(1), at(-2), at(2)
                br = 8.0 * (s1 - n1) - (s2 - n2)
                bc = c[:, 0:128]
                if target is None:
                    M3[p, j, here] = PS[STEPS, j, here] * br
                    N3[p, j, here] = PS[STEPS, j, here] * bc
                    continue
                BR[k, p, j, here] = br
                BC[k, p, j, here] = bc
                lap = (16.0 * (n1 + s1) - (n2 + s2)) + c[:, 128:256]
                target[p, j, here] = KEEP * at(0) + A * (
                    lap + AR[k, j, here] * br + AC[k, j, here] * bc
                )

        return body

    def spread(q_at, m_at, cross):
        s = q_at(-1) + q_at(1)
        ring = (s + s) + (m_at(-1) - m_at(1))
        outer = (q_at(-2) + q_at(2)) + (m_at(-2) - m_at(2))
        return KEEP * q_at(0) + A * ((8.0 * ring - outer) + cross)

    def p_flux(region):
        start, rows = region
        here = pl.ds(start, rows)
        for j in range(TILES):
            x = PP[STEPS, j, here]
            PS[STEPS, j, here] = SLOPE * x
            MP[STEPS, j, here] = x * AR[STEPS - 1, j, here]

    def p_step(k, region):
        start, rows = region
        here = pl.ds(start, rows)
        now = [PP[k + 1, j, here] for j in range(TILES)]
        cross = along([[x, x * AC[k, j, here]] for j, x in enumerate(now)], WK[...])
        results = []
        for j in range(TILES):
            q_at = lambda d: PP[k + 1, j, pl.ds(start + d, rows)]
            m_at = lambda d: MP[k + 1, j, pl.ds(start + d, rows)]
            out = spread(q_at, m_at, cross[j])
            if k > 0:
                PP[k, j, here] = out
                PS[k, j, here] = SLOPE * out
                MP[k, j, here] = out * AR[k - 1, j, here]
            results.append(out)
        if k == 0:
            to_natural(p_out, (), results, start, rows)

    def to_natural(ref, lead, tiles, start, rows):
        lane = lanes(rows)
        moved = [left(t, s) for t, s in zip(tiles, (112, 88, 64, 40, 16))]
        first = pl.multiple_of(start - REACH, 16)
        for n, edge in enumerate((100, 76, 52, 28)):
            ref[(*lead, pl.ds(first, rows), slice(128 * n, 128 * n + 128))] = jnp.where(
                lane < edge, moved[n], moved[n + 1]
            )

    def q_first(region):
        start, rows = region
        here = pl.ds(start, rows)

        def body(pairs):
            cross = along([[N3[p, j, here]] for p, j in pairs], WK[256:512])
            for (p, j), c in zip(pairs, cross):
                m_at = lambda d: M3[p, j, pl.ds(start + d, rows)]
                out = A * ((8.0 * (m_at(-1) - m_at(1)) - (m_at(-2) - m_at(2))) + c)
                Q3[p, j, here] = out
                M2[p, j, here] = out * AR[2, j, here] + PS[3, j, here] * BR[2, p, j, here]

        return body

    def q_step(k, source, flux, target, next_flux, region):
        start, rows = region
        here = pl.ds(start, rows)

        def body(pairs):
            def operands(p, j):
                x = source[p, j, here]
                return [x, x * AC[k, j, here] + PS[k + 1, j, here] * BC[k, p, j, here]]

            cross = along([operands(p, j) for p, j in pairs], WK[...])
            results = []
            for (p, j), c in zip(pairs, cross):
                q_at = lambda d: source[p, j, pl.ds(start + d, rows)]
                m_at = lambda d: flux[p, j, pl.ds(start + d, rows)]
                out = spread(q_at, m_at, c)
                if target is not None:
                    target[p, j, here] = out
                if next_flux is not None:
                    next_flux[p, j, here] = out * AR[k - 1, j, here] + PS[k, j, here] * BR[k - 1, p, j, here]
                results.append(out)
            if target is None:
                for i in range(0, len(pairs), TILES):
                    to_natural(q_out, (pairs[i][0],), results[i : i + TILES], start, rows)

        return body

    def refresh(region):
        start, rows = region

        def body(pairs):
            here = pl.ds(start, rows)
            lane = lanes(rows)
            for p, j in pairs:
                x = Q2[p, j, here]
                if j > 0:
                    x = jnp.where(lane < 12, left(Q2[p, j - 1, here], -104), x)
                if j < TILES - 1:
                    x = jnp.where(lane >= 116, left(Q2[p, j + 1, here], 104), x)
                QR[p, j, here] = x
                M1[p, j, here] = x * AR[1, j, here] + PS[2, j, here] * BR[1, p, j, here]

        return body

    def shared(region):
        slopes(region)
        p_flux(region(8))
        for k in reversed(range(STEPS)):
            p_step(k, region(16 - 2 * k))

    def sweep(region, first, last, batch):
        run = functools.partial(over, first, last, batch)
        run(tangent(0, U0, U1, region(2)))
        run(tangent(1, U1, U2, region(4)))
        run(tangent(2, U2, U3, region(6)))
        run(tangent(3, U3, None, region(8)))
        run(q_first(region(10)))
        run(q_step(2, Q3, M2, Q2, None, region(12)))
        run(refresh(region(12)))
        run(q_step(1, QR, M1, Q1, M0, region(14)))
        run(q_step(0, Q1, M0, None, None, region(16)))

    def main_region(margin):
        rows = (80 - 2 * margin + 15) // 16 * 16
        if margin == 16:
            return pl.multiple_of(32 - 16 * core, 16), rows
        return (1 - core) * (SPAN - margin - rows) + core * margin, rows

    load_own()

    @pl.when((late == 0) & (gx > 0))
    def _():
        early_sends()

    for c in near_u + [near_h] + near_k + side_c:
        c.wait_recv()
    own_sides()
    load_halo(near_halo, range(9))
    shared(main_region)

    @pl.when(gx == 0)
    def _():
        early_sends()

    sweep(main_region, 0, PROBES, 5)

    def wedge_region(margin):
        if margin == 16:
            return pl.multiple_of(16 + 48 * core, 16), REACH
        return (1 - core) * margin + core * (80 - margin), REACH

    far_h.wait_recv()
    for c in far_k:
        c.wait_recv()
    load_halo(far_halo, range(4, 9))
    shared(wedge_region)
    for c in far_u:
        c.wait_recv()
    load_halo(far_halo, range(4))
    sweep(wedge_region, 0, PROBES, 10)

    for c in far_u + [far_h] + far_k + near_u + [near_h] + near_k + side_c:
        c.wait_send()


def store_all(q, p, q_out, p_out, sem):
    copies = [
        pltpu.make_async_copy(q, q_out, sem.at[0]),
        pltpu.make_async_copy(p, p_out, sem.at[1]),
    ]
    for c in copies:
        c.start()
    for c in copies:
        c.wait()


def on_device(heights, probes, cotangent):
    f32 = jnp.float32
    probe = pltpu.VMEM((PROBES, TILES, SPAN, 128), f32)
    steps = pltpu.VMEM((STEPS + 1, TILES, SPAN, 128), f32)
    slope = pltpu.VMEM((3, PROBES, TILES, SPAN, 128), f32)
    q, p = pl.pallas_call(
        kernel,
        out_shape=[pltpu.VMEM((PROBES, ROWS, COLS), f32), pltpu.VMEM((ROWS, COLS), f32)],
        in_specs=[pl.BlockSpec(memory_space=pl.ANY)] * 3,
        out_specs=[pl.BlockSpec(memory_space=pltpu.VMEM)] * 2,
        scratch_shapes=[
            pltpu.VMEM((STEPS, ROWS, COLS), jnp.bfloat16),
            pltpu.VMEM((PROBES, ROWS, COLS), f32),
            pltpu.VMEM((ROWS, COLS), f32),
            pltpu.VMEM((2, 4, 72, 128), f32),
            pltpu.VMEM((2, PROBES, REACH, COLS), f32),
            pltpu.VMEM((2, 4, 72, 128), f32),
            pltpu.VMEM((2, ROWS, 128), f32),
            pltpu.VMEM((2, SPAN, 128), f32),
            probe,
            probe, probe, probe, probe,
            probe, probe,
            slope, slope,
            steps, steps, steps,
            probe, probe, probe, probe, probe, probe, probe, probe, probe,
            pltpu.VMEM((256, 256), jnp.bfloat16),
            pltpu.VMEM((512, 128), jnp.bfloat16),
            pltpu.SemaphoreType.DMA((3,)),
            pltpu.SemaphoreType.DMA((16,)),
            pltpu.SemaphoreType.DMA((16,)),
            pltpu.SemaphoreType.REGULAR((5,)),
        ],
        compiler_params=pltpu.CompilerParams(
            collective_id=0, has_side_effects=True, vmem_limit_bytes=56 * 2**20
        ),
    )(heights, probes, cotangent)
    return pl.pallas_call(
        store_all,
        out_shape=[jax.ShapeDtypeStruct(q.shape, f32), jax.ShapeDtypeStruct(p.shape, f32)],
        in_specs=[pl.BlockSpec(memory_space=pltpu.VMEM)] * 2,
        out_specs=[pl.BlockSpec(memory_space=pl.ANY)] * 2,
        scratch_shapes=[pltpu.SemaphoreType.DMA((2,))],
    )(
        pltpu.with_memory_space_constraint(q, pltpu.VMEM),
        pltpu.with_memory_space_constraint(p, pltpu.VMEM),
    )


def solution(mesh):
    in_specs = (P(None, "gx", "gy"), P(None, "gx", "gy"), P("gx", "gy"))
    out_specs = (P(None, "gx", "gy"), P("gx", "gy"))
    return jax.shard_map(
        on_device, mesh=mesh, in_specs=in_specs, out_specs=out_specs, check_vma=False
    )
```

time: 35.6 us -> 22.3 us (0.63)
  Pallas kernels: 32.3 us -> 21.5 us
  local copies, waits for them, and re-layouts: 2.56 us -> 0 us
    pallas_call x1 -> x2, Pallas kernels: 32.3 us -> 21.5 us  [the longest x1 20.7 us: on_device(): pl.pallas_call(kernel, out_shape=[pltpu.VMEM((PROBES, ROWS, COLS), f32),...]
    unnamed x4 -> x0, local copies, waits for them, and re-layouts: 2.56 us -> none
where the time goes in v2:
time: 22.3 us; the launch traced here: 22.2 us
  Pallas kernels  21.5 us (96%)
  between operations  0.64 us (3%)
    pallas_call x1, Pallas kernels, on_device(): pl.pallas_call(kernel, out_shape=[pltpu.VMEM((PROBES, ROWS, COLS), f32),...  20.7 us
    pallas_call x1, Pallas kernels, on_device(): pl.pallas_call(store_all, out_shape=[jax.ShapeDtypeStruct(q.shape, f32),...  0.85 us

profile of v2, /device:TPU:4, one launch (start us, length us, event | category | flops | bytes accessed | tf_op | source)
XLA Modules:
  0.0 22.2 jit_solution(5349382989312180201)
XLA Ops:
  0.6 20.7 %shard_map.50 = (f32[4,64,512]{2,1,0:T(8,128)S(1)}, f32[64,512]{1,0:T(8,128)S(1)}) custom-call(bf16[4,64,512]{2,1,0:T(8,128)(2,1)} %heights.1, f32[4,64,512]{2,1,0:T(8,128)} %probes.1, f32[64,512]{1,0:T(8,128)} %cotangent.1), custom_call_target="tpu_custom_call" | custom-call | tf_op jit(solution)/shard_map/pallas_call | solution.py:508
  21.3 0.8 %shard_map.51 = (f32[4,64,512]{2,1,0:T(8,128)}, f32[64,512]{1,0:T(8,128)}) custom-call(f32[4,64,512]{2,1,0:T(8,128)S(1)} %get-tuple-element.4.q, f32[64,512]{1,0:T(8,128)S(1)} %get-tuple-element.5.p), custom_call_target="tpu_custom_call" | custom-call | tf_op jit(solution)/shard_map/pallas_call | solution.py:539

commit v3 on v2

--- a/solution.py
+++ b/solution.py
@@ -44,36 +44,36 @@
     gx, gy = lax.axis_index("gx"), lax.axis_index("gy")
     n_gx, n_gy = lax.axis_size("gx"), lax.axis_size("gy")
     core = lax.rem(gx, 2)
-    late = lax.rem(lax.div(gx, 2), 2)
     near_gx = gx + 1 - 2 * core
     far_gx = lax.rem(gx - 1 + 2 * core + n_gx, n_gx)
     west, east = lax.rem(gy + n_gy - 1, n_gy), lax.rem(gy + 1, n_gy)
-    y = lax.rem(gy, 4)
 
     def signal(sem, device):
         pl.semaphore_signal(sem, inc=1, device_id=device, device_id_type=MESH)
 
-    greets_far, greets_near, greets_west, greets_east = late == 0, core == 1, y == 0, y < 3
+    first_row, last_row = gx == 0, gx == n_gx - 1
+    y = lax.rem(gy, 4)
+    asks_west = last_row & (y == 0)
+    answers = [last_row & (y == 3), (gx == n_gx - 2) & (y == 3)]
     barrier = pltpu.get_barrier_semaphore()
-    far_corners = [(far_gx, west), (far_gx, east)]
-
-    @pl.when(greets_near)
-    def _():
-        signal(barrier, (near_gx, gy))
-
-    @pl.when(greets_far)
-    def _():
-        for d in [(far_gx, gy)] + far_corners:
+    far, western, eastern = (far_gx, gy), [(gx, west), (near_gx, west)], [(gx, east), (near_gx, east)]
+    corners = [(far_gx, west), (far_gx, east)]
+
+    @pl.when(jnp.logical_not(last_row))
+    def _():
+        signal(barrier, far)
+
+    @pl.when(first_row)
+    def _():
+        for d in corners:
             signal(barrier, d)
 
-    @pl.when(greets_east)
-    def _():
-        for d in [(gx, east), (near_gx, east)]:
-            signal(barrier, d)
-
-    @pl.when(greets_west)
-    def _():
-        for d in [(gx, west), (near_gx, west)]:
+    for d in [(near_gx, gy)] + western:
+        signal(barrier, d)
+    for d, special in zip(eastern, answers):
+
+        @pl.when(jnp.logical_not(special))
+        def _():
             signal(barrier, d)
 
     loads = [
@@ -121,65 +121,33 @@
     def c_copy(side, s, d):
         return copy(send_cols.at[side], cols.at[1 - side, pl.ds(REACH, ROWS)], s, d)
 
-    def k_copy(side, edge, s, d):
+    def k_copy(side, s, d):
         return copy(
-            send_cols.at[side, pl.ds(row_start(edge), REACH)],
-            cols.at[1 - side, pl.ds(halo_start(1 - edge), REACH)], s, d,
+            send_cols.at[side, pl.ds(row_start(near_edge), REACH)],
+            cols.at[1 - side, pl.ds(halo_start(1 - near_edge), REACH)], s, d,
         )
 
-    far_u = [u_copy(far_edge, p, p, (far_gx, gy)) for p in range(PROBES)]
-    far_h = h_copy(far_edge, 4, (far_gx, gy))
-    far_k = [k_copy(side, far_edge, 5 + side, far_corners[side]) for side in (0, 1)]
+    def direct(side, s):
+        return copy(
+            send_cols.at[side, pl.ds(row_start(far_edge), REACH)],
+            cols.at[1 - side, pl.ds(halo_start(1 - far_edge), REACH)], s, corners[side],
+        )
+
+    def pass_on(side, s):
+        return copy(
+            cols.at[side, pl.ds(pl.multiple_of(REACH + row_start(far_edge), 16), REACH)],
+            cols.at[side, pl.ds(halo_start(1 - far_edge), REACH)], s, far,
+        )
+
+    far_u = [u_copy(far_edge, p, p, far) for p in range(PROBES)]
+    far_h = h_copy(far_edge, 4, far)
+    far_k = [pass_on(side, 5 + side) for side in (0, 1)]
+    direct_k = [direct(side, 5 + side) for side in (0, 1)]
     near_u = [u_copy(near_edge, p, 7 + p, (near_gx, gy)) for p in range(PROBES)]
     near_h = h_copy(near_edge, 11, (near_gx, gy))
-    near_k = [k_copy(0, near_edge, 12, (near_gx, west)), k_copy(1, near_edge, 13, (near_gx, east))]
-    side_c = [c_copy(0, 14, (gx, west)), c_copy(1, 15, (gx, east))]
-
-    greeters = 3 * late + (1 - core) + jnp.where(y > 0, 2, 0) + jnp.where(y == 3, 2, 0)
-
-    @pl.when(greeters > 0)
-    def _():
-        pl.semaphore_wait(barrier, greeters)
-
-
-    @pl.when(late == 1)
-    def _():
-        for c in far_u[:2]:
-            c.start()
-        signal(answer.at[0], (far_gx, gy))
-        for d in far_corners:
-            signal(answer.at[1], d)
-
-    @pl.when(core == 0)
-    def _():
-        signal(answer.at[2], (near_gx, gy))
-
-    @pl.when(y > 0)
-    def _():
-        for d in [(gx, west), (near_gx, west)]:
-            signal(answer.at[4], d)
-
-    @pl.when(y == 3)
-    def _():
-        for d in [(gx, east), (near_gx, east)]:
-            signal(answer.at[3], d)
-
-    def answered(greeted, which, count):
-        @pl.when(greeted)
-        def _():
-            pl.semaphore_wait(answer.at[which], count)
-
-    def early_sends():
-        pl.semaphore_wait(answer.at[0], 1)
-        for c in far_u[:2] + [far_h] + far_u[2:]:
-            c.start()
-        pl.semaphore_wait(answer.at[1], 2)
-        for c in far_k:
-            c.start()
-
-    answered(greets_near, 2, 1)
-    for c in near_u:
-        c.start()
+    near_k = [k_copy(0, 12, western[1]), k_copy(1, 13, eastern[1])]
+    side_c = [c_copy(0, 14, western[0]), c_copy(1, 15, eastern[0])]
+    bulk = far_u[:2] + [far_h] + far_u[2:]
 
     loads[0].wait()
     loads[1].wait()
@@ -192,7 +160,6 @@
             first = PACK_ROWS[k] - 2 * k
             send_rows[1, n, first : first + 16] = hb[k, 48:64, cut].astype(jnp.float32)
         send_rows[1, n, 52:60] = cb[56:64, cut]
-    near_h.start()
 
     loads[2].wait()
     lane = lanes(ROWS)
@@ -209,73 +176,83 @@
             x = left(x, o if side == 0 else o + w)
             packed = x if packed is None else jnp.where(lane < o, packed, x)
         send_cols[side] = packed
-    for side, greeted in ((0, greets_west), (1, greets_east)):
-        answered(greeted, 3 + side, 2)
-        for c in (side_c[side], near_k[side]):
+
+    pl.semaphore_wait(barrier, 5 + jnp.where(first_row, 0, jnp.where(last_row, 3, 1)) - jnp.where(asks_west, 2, 0))
+
+    @pl.when(last_row)
+    def _():
+        for d in [far] + corners:
+            signal(answer.at[0], d)
+        for c in direct_k:
             c.start()
 
-    @pl.when(late == 1)
-    def _():
-        for c in far_k + [far_h] + far_u[2:]:
+    for d, special in zip(eastern, answers):
+
+        @pl.when(special)
+        def _():
+            signal(answer.at[1], d)
+
+    for c in near_u + [near_h, side_c[1], near_k[1]]:
+        c.start()
+
+    @pl.when(jnp.logical_not(asks_west))
+    def _():
+        for c in [side_c[0], near_k[0]]:
+            c.start()
+
+    @pl.when(jnp.logical_not(first_row))
+    def _():
+        for c in bulk:
             c.start()
 
     def inner_tiles(store, nat, rows):
         lane = lanes(rows)
         for j, shift in ((1, 40), (2, 64), (3, 88)):
             store(j, jnp.where(lane < shift, left(nat[j - 1], shift), left(nat[j], shift)))
-        return left(nat[0], 16), left(nat[3], 112)
 
     def outer_tiles(store, first, last, before, after, f, rows):
         lane = lanes(rows)
         w, o = WIDTHS[f], LANES[f]
-        store(0, jnp.where(lane < 16, left(before, 16 - w - o), first))
-        store(4, jnp.where(lane < 112, last, left(after, 112 - o)))
-
-    def place(f):
-        return (U0, (f,)) if f < 4 else (H, (f - 4,)) if f < 8 else (PP, (4,))
+        store(0, jnp.where(lane < 16, left(before, 16 - w - o), left(first, 16)))
+        store(4, jnp.where(lane < 112, left(last, 112), left(after, 112 - o)))
 
     def put(f, start, rows):
-        ref, lead = place(f)
+        ref, lead = (U0, (f,)) if f < 4 else (H, (f - 4,)) if f < 8 else (PP, (4,))
 
         def store(j, value):
             ref[(*lead, j, pl.ds(start, rows))] = value
 
         return store
 
-    def load_own():
+    def own(f, n):
+        cut = slice(128 * n, 128 * n + 128)
+        return ub[f, :, cut] if f < 4 else hb[f - 4, :, cut].astype(jnp.float32) if f < 8 else cb[:, cut]
+
+    def lay_own(inner):
         for f in range(9):
-            cuts = [slice(128 * n, 128 * n + 128) for n in range(4)]
-            if f < 4:
-                nat = [ub[f, :, cut] for cut in cuts]
-            elif f < 8:
-                nat = [hb[f - 4, :, cut].astype(jnp.float32) for cut in cuts]
+            store = put(f, REACH, ROWS)
+            if inner:
+                inner_tiles(store, [own(f, n) for n in range(4)], ROWS)
             else:
-                nat = [cb[:, cut] for cut in cuts]
-            store = put(f, REACH, ROWS)
-            first, last = inner_tiles(store, nat, ROWS)
-            store(0, first)
-            store(4, last)
-
-    def own_sides():
-        before, after = cols[0, REACH : REACH + ROWS], cols[1, REACH : REACH + ROWS]
-        for f in range(9):
-            ref, lead = place(f)
-            mine = slice(REACH, REACH + ROWS)
-            outer_tiles(put(f, REACH, ROWS), ref[(*lead, 0, mine)], ref[(*lead, 4, mine)], before, after, f, ROWS)
-
-    def load_halo(halo, fields):
+                mine = slice(REACH, REACH + ROWS)
+                outer_tiles(store, own(f, 0), own(f, 3), cols[0, mine], cols[1, mine], f, ROWS)
+
+    def lay_halo(halo, fields, inner, outer):
         start = halo_start(halo)
-        before, after = cols[0, pl.ds(start, REACH)], cols[1, pl.ds(start, REACH)]
         for f in fields:
-            if f < 4:
-                nat = [rows_u[halo, f, :, 128 * n : 128 * n + 128] for n in range(4)]
-            else:
+
+            def part(n):
+                if f < 4:
+                    return rows_u[halo, f, :, 128 * n : 128 * n + 128]
                 k = f - 4
-                first = PACK_ROWS[k] - (1 - halo) * (2 * k)
-                nat = [rows_h[halo, n, pl.ds(first, REACH)] for n in range(4)]
+                return rows_h[halo, n, pl.ds(PACK_ROWS[k] - (1 - halo) * (2 * k), REACH)]
+
             store = put(f, start, REACH)
-            first, last = inner_tiles(store, nat, REACH)
-            outer_tiles(store, first, last, before, after, f, REACH)
+            if inner:
+                inner_tiles(store, [part(n) for n in range(4)], REACH)
+            if outer:
+                sides = [cols[side, pl.ds(start, REACH)] for side in (0, 1)]
+                outer_tiles(store, part(0), part(3), *sides, f, REACH)
 
     def dot(x, w):
         return jnp.dot(x, w, preferred_element_type=jnp.float32)
@@ -290,19 +267,19 @@
         out = dot(jnp.concatenate(stacked, axis=0), w)
         return [out[i * rows : i * rows + rows] for i in range(len(columns))]
 
-    def slopes(region):
+    def slopes(region, tiles):
         for k in range(STEPS):
             start, rows = region(2 * k + 2)
             here = pl.ds(start, rows)
-            whole = jnp.concatenate([H[k, j, here].astype(jnp.bfloat16) for j in range(TILES)], axis=0)
+            whole = jnp.concatenate([H[k, j, here].astype(jnp.bfloat16) for j in tiles], axis=0)
             cross = dot(whole, W[0:128, 0:128])
-            for j in range(TILES):
+            for i, j in enumerate(tiles):
                 at = lambda d: H[k, j, pl.ds(start + d, rows)]
                 AR[k, j, here] = SLOPE * (8.0 * (at(1) - at(-1)) - (at(2) - at(-2)))
-                AC[k, j, here] = SLOPE * cross[j * rows : j * rows + rows]
-
-    def over(first, last, batch, body):
-        pairs = [(p, j) for p in range(first, last) for j in range(TILES)]
+                AC[k, j, here] = SLOPE * cross[i * rows : i * rows + rows]
+
+    def over(probes_of, tiles, batch, body):
+        pairs = [(p, j) for p in probes_of for j in tiles]
         for i in range(0, len(pairs), batch):
             body(pairs[i : i + batch])
 
@@ -336,24 +313,23 @@
         outer = (q_at(-2) + q_at(2)) + (m_at(-2) - m_at(2))
         return KEEP * q_at(0) + A * ((8.0 * ring - outer) + cross)
 
-    def p_flux(region):
+    def p_flux(region, tiles):
         start, rows = region
         here = pl.ds(start, rows)
-        for j in range(TILES):
+        for j in tiles:
             x = PP[STEPS, j, here]
             PS[STEPS, j, here] = SLOPE * x
             MP[STEPS, j, here] = x * AR[STEPS - 1, j, here]
 
-    def p_step(k, region):
+    def p_step(k, region, tiles):
         start, rows = region
         here = pl.ds(start, rows)
-        now = [PP[k + 1, j, here] for j in range(TILES)]
-        cross = along([[x, x * AC[k, j, here]] for j, x in enumerate(now)], WK[...])
+        cross = along([[PP[k + 1, j, here], PP[k + 1, j, here] * AC[k, j, here]] for j in tiles], WK[...])
         results = []
-        for j in range(TILES):
+        for j, c in zip(tiles, cross):
             q_at = lambda d: PP[k + 1, j, pl.ds(start + d, rows)]
             m_at = lambda d: MP[k + 1, j, pl.ds(start + d, rows)]
-            out = spread(q_at, m_at, cross[j])
+            out = spread(q_at, m_at, c)
             if k > 0:
                 PP[k, j, here] = out
                 PS[k, j, here] = SLOPE * out
@@ -428,20 +404,25 @@
 
         return body
 
-    def shared(region):
-        slopes(region)
-        p_flux(region(8))
-        for k in reversed(range(STEPS)):
-            p_step(k, region(16 - 2 * k))
-
-    def sweep(region, first, last, batch):
-        run = functools.partial(over, first, last, batch)
+    everyone, all_tiles = tuple(range(PROBES)), range(TILES)
+
+    def shared(region, tiles):
+        slopes(region, tiles)
+        p_flux(region(8), tiles)
+        for k in (3, 2, 1):
+            p_step(k, region(16 - 2 * k), tiles)
+
+    def sweep(region, tiles, batch, which=everyone):
+        run = functools.partial(over, which, tiles, batch)
         run(tangent(0, U0, U1, region(2)))
         run(tangent(1, U1, U2, region(4)))
         run(tangent(2, U2, U3, region(6)))
         run(tangent(3, U3, None, region(8)))
         run(q_first(region(10)))
         run(q_step(2, Q3, M2, Q2, None, region(12)))
+
+    def finish(region, batch, which=everyone):
+        run = functools.partial(over, which, all_tiles, batch)
         run(refresh(region(12)))
         run(q_step(1, QR, M1, Q1, M0, region(14)))
         run(q_step(0, Q1, M0, None, None, region(16)))
@@ -452,23 +433,42 @@
             return pl.multiple_of(32 - 16 * core, 16), rows
         return (1 - core) * (SPAN - margin - rows) + core * margin, rows
 
-    load_own()
-
-    @pl.when((late == 0) & (gx > 0))
-    def _():
-        early_sends()
-
-    for c in near_u + [near_h] + near_k + side_c:
+    lay_own(True)
+
+    @pl.when(asks_west)
+    def _():
+        pl.semaphore_wait(answer.at[1], 2)
+        for c in [side_c[0], near_k[0]]:
+            c.start()
+
+    for c in near_u + [near_h]:
         c.wait_recv()
-    own_sides()
-    load_halo(near_halo, range(9))
-    shared(main_region)
-
-    @pl.when(gx == 0)
-    def _():
-        early_sends()
-
-    sweep(main_region, 0, PROBES, 5)
+    lay_halo(near_halo, range(9), True, False)
+    shared(main_region, (1, 2, 3))
+    sweep(main_region, (1, 2, 3), 6)
+
+    @pl.when(first_row)
+    def _():
+        pl.semaphore_wait(answer.at[0], 3)
+        for c in direct_k + bulk:
+            c.start()
+
+    for c in side_c:
+        c.wait_recv()
+
+    @pl.when(jnp.logical_not(first_row | last_row))
+    def _():
+        for c in far_k:
+            c.start()
+
+    lay_own(False)
+    for c in near_k:
+        c.wait_recv()
+    lay_halo(near_halo, range(9), False, True)
+    shared(main_region, (0, 4))
+    sweep(main_region, (0, 4), 4)
+    p_step(0, main_region(16), all_tiles)
+    finish(main_region, 5)
 
     def wedge_region(margin):
         if margin == 16:
@@ -478,12 +478,14 @@
     far_h.wait_recv()
     for c in far_k:
         c.wait_recv()
-    load_halo(far_halo, range(4, 9))
-    shared(wedge_region)
+    lay_halo(far_halo, range(4, 9), True, True)
+    shared(wedge_region, all_tiles)
+    p_step(0, wedge_region(16), all_tiles)
     for c in far_u:
         c.wait_recv()
-    load_halo(far_halo, range(4))
-    sweep(wedge_region, 0, PROBES, 10)
+    lay_halo(far_halo, everyone, True, True)
+    sweep(wedge_region, all_tiles, 10)
+    finish(wedge_region, 10)
 
     for c in far_u + [far_h] + far_k + near_u + [near_h] + near_k + side_c:
         c.wait_send()
@@ -530,7 +532,7 @@
             pltpu.SemaphoreType.DMA((3,)),
             pltpu.SemaphoreType.DMA((16,)),
             pltpu.SemaphoreType.DMA((16,)),
-            pltpu.SemaphoreType.REGULAR((5,)),
+            pltpu.SemaphoreType.REGULAR((2,)),
         ],
         compiler_params=pltpu.CompilerParams(
             collective_id=0, has_side_effects=True, vmem_limit_bytes=56 * 2**20

time: 22.3 us -> 20.5 us (0.919)
  the two profiles are of different devices: /device:TPU:4 before, /device:TPU:1 now
where the time goes in v3:
time: 20.5 us; the launch traced here: 20.3 us
  Pallas kernels  19.7 us (96%)
  between operations  0.64 us (3%)
    pallas_call x1, Pallas kernels, on_device(): pl.pallas_call(kernel, out_shape=[pltpu.VMEM((PROBES, ROWS, COLS), f32),...  18.8 us
    pallas_call x1, Pallas kernels, on_device(): pl.pallas_call(store_all, out_shape=[jax.ShapeDtypeStruct(q.shape, f32),...  0.85 us

profile of v3, /device:TPU:1, one launch (start us, length us, event | category | flops | bytes accessed | tf_op | source)
XLA Modules:
  0.0 20.3 jit_solution(16329258947616182700)
XLA Ops:
  0.6 18.8 %shard_map.50 = (f32[4,64,512]{2,1,0:T(8,128)S(1)}, f32[64,512]{1,0:T(8,128)S(1)}) custom-call(bf16[4,64,512]{2,1,0:T(8,128)(2,1)} %heights.1, f32[4,64,512]{2,1,0:T(8,128)} %probes.1, f32[64,512]{1,0:T(8,128)} %cotangent.1), custom_call_target="tpu_custom_call" | custom-call | tf_op jit(solution)/shard_map/pallas_call | solution.py:510
  19.5 0.8 %shard_map.51 = (f32[4,64,512]{2,1,0:T(8,128)}, f32[64,512]{1,0:T(8,128)}) custom-call(f32[4,64,512]{2,1,0:T(8,128)S(1)} %get-tuple-element.4.q, f32[64,512]{1,0:T(8,128)S(1)} %get-tuple-element.5.p), custom_call_target="tpu_custom_call" | custom-call | tf_op jit(solution)/shard_map/pallas_call | solution.py:541

commit v4 on v3

--- a/solution.py
+++ b/solution.py
@@ -29,6 +29,10 @@
 
 def left(x, by):
     return pltpu.roll(x, by % 128, 1)
+
+
+def aligned(x):
+    return x if isinstance(x, int) else pl.multiple_of(x, 16)
 
 
 def lanes(rows):
@@ -53,8 +57,12 @@
 
     first_row, last_row = gx == 0, gx == n_gx - 1
     y = lax.rem(gy, 4)
-    asks_west = last_row & (y == 0)
-    answers = [last_row & (y == 3), (gx == n_gx - 2) & (y == 3)]
+    place_of_four = jnp.where(gx < n_gx - 2, lax.rem(gx, 4), -1)
+    asks_west = (last_row | (place_of_four == 2)) & (y == 0)
+    answers = [
+        (last_row | (place_of_four == 2)) & (y == 3),
+        ((gx == n_gx - 2) | (place_of_four == 3)) & (y == 3),
+    ]
     barrier = pltpu.get_barrier_semaphore()
     far, western, eastern = (far_gx, gy), [(gx, west), (near_gx, west)], [(gx, east), (near_gx, east)]
     corners = [(far_gx, west), (far_gx, east)]
@@ -97,8 +105,6 @@
     WK[256:512] = taps(256, -8.0, 1.0, -1.0)
 
     near_edge, far_edge = 1 - core, core
-    near_halo, far_halo = 1 - core, core
-
     def copy(src, dst, s, d):
         return pltpu.make_async_remote_copy(
             src_ref=src, dst_ref=dst, send_sem=send_sem.at[s], recv_sem=recv_sem.at[s],
@@ -109,10 +115,10 @@
         return pl.multiple_of(edge * (ROWS - REACH), 16)
 
     def halo_start(halo):
-        return pl.multiple_of(halo * (SPAN - REACH), 16)
+        return aligned(halo * (SPAN - REACH))
 
     def u_copy(edge, p, s, d):
-        return copy(probes.at[p, pl.ds(row_start(edge), REACH)], rows_u.at[1 - edge, p], s, d)
+        return copy(ub.at[p, pl.ds(row_start(edge), REACH)], rows_u.at[1 - edge, p], s, d)
 
     def h_copy(edge, s, d):
         part = (slice(None), pl.ds(0, 64))
@@ -261,11 +267,28 @@
         high = x.astype(jnp.bfloat16)
         return [high, (x - high.astype(jnp.float32)).astype(jnp.bfloat16)]
 
-    def along(columns, w):
+    def along(columns, kind):
         rows = columns[0][0].shape[0]
+        if rows == REACH:
+            return [along_rolled(xs, kind) for xs in columns]
+        w = {"both": W[...], "slope": W[:, 0:128], "minus": WK[256:512], "step": WK[...]}[kind]
         stacked = [jnp.concatenate(sum([halves(x) for x in xs], []), axis=1) for xs in columns]
         out = dot(jnp.concatenate(stacked, axis=0), w)
         return [out[i * rows : i * rows + rows] for i in range(len(columns))]
+
+    def along_rolled(xs, kind):
+        x = xs[0]
+        if kind == "step":
+            my, two = xs[1], x + x
+            ring = left(two + my, 1) + left(two - my, -1)
+            return 8.0 * ring - (left(x + my, 2) + left(x - my, -2))
+        w1, e1, w2, e2 = left(x, 1), left(x, -1), left(x, 2), left(x, -2)
+        if kind == "minus":
+            return 8.0 * (w1 - e1) - (w2 - e2)
+        slope = 8.0 * (e1 - w1) - (e2 - w2)
+        if kind == "slope":
+            return slope
+        return jnp.concatenate([slope, 16.0 * (e1 + w1) - (e2 + w2)], axis=1)
 
     def slopes(region, tiles):
         for k in range(STEPS):
@@ -288,7 +311,7 @@
         here = pl.ds(start, rows)
 
         def body(pairs):
-            cross = along([[source[p, j, here]] for p, j in pairs], W[:, 0:128] if target is None else W[...])
+            cross = along([[source[p, j, here]] for p, j in pairs], "slope" if target is None else "both")
             for (p, j), c in zip(pairs, cross):
                 at = lambda d: source[p, j, pl.ds(start + d, rows)]
                 n1, s1, n2, s2 = at(-1), at(1), at(-2), at(2)
@@ -324,7 +347,7 @@
     def p_step(k, region, tiles):
         start, rows = region
         here = pl.ds(start, rows)
-        cross = along([[PP[k + 1, j, here], PP[k + 1, j, here] * AC[k, j, here]] for j in tiles], WK[...])
+        cross = along([[PP[k + 1, j, here], PP[k + 1, j, here] * AC[k, j, here]] for j in tiles], "step")
         results = []
         for j, c in zip(tiles, cross):
             q_at = lambda d: PP[k + 1, j, pl.ds(start + d, rows)]
@@ -341,7 +364,7 @@
     def to_natural(ref, lead, tiles, start, rows):
         lane = lanes(rows)
         moved = [left(t, s) for t, s in zip(tiles, (112, 88, 64, 40, 16))]
-        first = pl.multiple_of(start - REACH, 16)
+        first = aligned(start - REACH)
         for n, edge in enumerate((100, 76, 52, 28)):
             ref[(*lead, pl.ds(first, rows), slice(128 * n, 128 * n + 128))] = jnp.where(
                 lane < edge, moved[n], moved[n + 1]
@@ -352,7 +375,7 @@
         here = pl.ds(start, rows)
 
         def body(pairs):
-            cross = along([[N3[p, j, here]] for p, j in pairs], WK[256:512])
+            cross = along([[N3[p, j, here]] for p, j in pairs], "minus")
             for (p, j), c in zip(pairs, cross):
                 m_at = lambda d: M3[p, j, pl.ds(start + d, rows)]
                 out = A * ((8.0 * (m_at(-1) - m_at(1)) - (m_at(-2) - m_at(2))) + c)
@@ -370,7 +393,7 @@
                 x = source[p, j, here]
                 return [x, x * AC[k, j, here] + PS[k + 1, j, here] * BC[k, p, j, here]]
 
-            cross = along([operands(p, j) for p, j in pairs], WK[...])
+            cross = along([operands(p, j) for p, j in pairs], "step")
             results = []
             for (p, j), c in zip(pairs, cross):
                 q_at = lambda d: source[p, j, pl.ds(start + d, rows)]
@@ -409,14 +432,15 @@
     def shared(region, tiles):
         slopes(region, tiles)
         p_flux(region(8), tiles)
-        for k in (3, 2, 1):
-            p_step(k, region(16 - 2 * k), tiles)
 
     def sweep(region, tiles, batch, which=everyone):
         run = functools.partial(over, which, tiles, batch)
         run(tangent(0, U0, U1, region(2)))
+        p_step(3, region(10), tiles)
         run(tangent(1, U1, U2, region(4)))
+        p_step(2, region(12), tiles)
         run(tangent(2, U2, U3, region(6)))
+        p_step(1, region(14), tiles)
         run(tangent(3, U3, None, region(8)))
         run(q_first(region(10)))
         run(q_step(2, Q3, M2, Q2, None, region(12)))
@@ -424,14 +448,9 @@
     def finish(region, batch, which=everyone):
         run = functools.partial(over, which, all_tiles, batch)
         run(refresh(region(12)))
+        p_step(0, region(16), all_tiles)
         run(q_step(1, QR, M1, Q1, M0, region(14)))
         run(q_step(0, Q1, M0, None, None, region(16)))
-
-    def main_region(margin):
-        rows = (80 - 2 * margin + 15) // 16 * 16
-        if margin == 16:
-            return pl.multiple_of(32 - 16 * core, 16), rows
-        return (1 - core) * (SPAN - margin - rows) + core * margin, rows
 
     lay_own(True)
 
@@ -441,51 +460,62 @@
         for c in [side_c[0], near_k[0]]:
             c.start()
 
-    for c in near_u + [near_h]:
-        c.wait_recv()
-    lay_halo(near_halo, range(9), True, False)
-    shared(main_region, (1, 2, 3))
-    sweep(main_region, (1, 2, 3), 6)
-
-    @pl.when(first_row)
-    def _():
-        pl.semaphore_wait(answer.at[0], 3)
-        for c in direct_k + bulk:
-            c.start()
-
-    for c in side_c:
-        c.wait_recv()
-
-    @pl.when(jnp.logical_not(first_row | last_row))
-    def _():
-        for c in far_k:
-            c.start()
-
-    lay_own(False)
-    for c in near_k:
-        c.wait_recv()
-    lay_halo(near_halo, range(9), False, True)
-    shared(main_region, (0, 4))
-    sweep(main_region, (0, 4), 4)
-    p_step(0, main_region(16), all_tiles)
-    finish(main_region, 5)
-
-    def wedge_region(margin):
-        if margin == 16:
-            return pl.multiple_of(16 + 48 * core, 16), REACH
-        return (1 - core) * margin + core * (80 - margin), REACH
-
-    far_h.wait_recv()
-    for c in far_k:
-        c.wait_recv()
-    lay_halo(far_halo, range(4, 9), True, True)
-    shared(wedge_region, all_tiles)
-    p_step(0, wedge_region(16), all_tiles)
-    for c in far_u:
-        c.wait_recv()
-    lay_halo(far_halo, everyone, True, True)
-    sweep(wedge_region, all_tiles, 10)
-    finish(wedge_region, 10)
+    def phases(core):
+        near_halo, far_halo = 1 - core, core
+
+        def main_region(margin):
+            rows = (80 - 2 * margin + 15) // 16 * 16
+            if margin == 16:
+                return aligned(32 - 16 * core), rows
+            return (1 - core) * (SPAN - margin - rows) + core * margin, rows
+
+        for c in near_u + [near_h]:
+            c.wait_recv()
+        lay_halo(near_halo, range(9), True, False)
+        shared(main_region, (1, 2, 3))
+        sweep(main_region, (1, 2, 3), 6)
+
+        @pl.when(first_row)
+        def _():
+            pl.semaphore_wait(answer.at[0], 3)
+            for c in direct_k + bulk:
+                c.start()
+
+        for c in side_c:
+            c.wait_recv()
+
+        @pl.when(jnp.logical_not(first_row | last_row))
+        def _():
+            for c in far_k:
+                c.start()
+
+        lay_own(False)
+        for c in near_k:
+            c.wait_recv()
+        lay_halo(near_halo, range(9), False, True)
+        shared(main_region, (0, 4))
+        sweep(main_region, (0, 4), 4)
+        finish(main_region, 5)
+
+        def wedge_region(margin):
+            if margin == 16:
+                return aligned(16 + 48 * core), REACH
+            return (1 - core) * margin + core * (80 - margin), REACH
+
+        for c in [far_h] + far_u + far_k:
+            c.wait_recv()
+        lay_halo(far_halo, range(9), True, True)
+        shared(wedge_region, all_tiles)
+        sweep(wedge_region, all_tiles, 5)
+        finish(wedge_region, 5)
+
+    @pl.when(core == 0)
+    def _():
+        phases(0)
+
+    @pl.when(core == 1)
+    def _():
+        phases(1)
 
     for c in far_u + [far_h] + far_k + near_u + [near_h] + near_k + side_c:
         c.wait_send()

time: 20.5 us -> 19.4 us (0.946)
  the two profiles are of different devices: /device:TPU:1 before, /device:TPU:8 now
where the time goes in v4:
time: 19.4 us; the launch traced here: 19.2 us
  Pallas kernels  18.4 us (95%)
  between operations  0.82 us (4%)
    pallas_call x1, Pallas kernels, on_device(): pl.pallas_call(kernel, out_shape=[pltpu.VMEM((PROBES, ROWS, COLS), f32),...  17.6 us
    pallas_call x1, Pallas kernels, on_device(): pl.pallas_call(store_all, out_shape=[jax.ShapeDtypeStruct(q.shape, f32),...  0.85 us

profile of v4, /device:TPU:8, one launch (start us, length us, event | category | flops | bytes accessed | tf_op | source)
XLA Modules:
  0.0 19.2 jit_solution(18215699607347252260)
XLA Ops:
  0.6 17.6 %shard_map.50 = (f32[4,64,512]{2,1,0:T(8,128)S(1)}, f32[64,512]{1,0:T(8,128)S(1)}) custom-call(bf16[4,64,512]{2,1,0:T(8,128)(2,1)} %heights.1, f32[4,64,512]{2,1,0:T(8,128)} %probes.1, f32[64,512]{1,0:T(8,128)} %cotangent.1), custom_call_target="tpu_custom_call" | custom-call | tf_op jit(solution)/shard_map/pallas_call | solution.py:540
  18.2 0.8 %shard_map.51 = (f32[4,64,512]{2,1,0:T(8,128)}, f32[64,512]{1,0:T(8,128)}) custom-call(f32[4,64,512]{2,1,0:T(8,128)S(1)} %get-tuple-element.4.q, f32[64,512]{1,0:T(8,128)S(1)} %get-tuple-element.5.p), custom_call_target="tpu_custom_call" | custom-call | tf_op jit(solution)/shard_map/pallas_call | solution.py:571
